TPU v7x, 128 devices: a whole 4x4x4 slice. The times are simulated.
128 devices in a mesh: dp: 8 (over y_hi, x), space: 16 (over z, y_lo, core).
Axes of the slice: x: 4, y: 4 (y_hi: 2, y_lo: 2; y = y_hi * 2 + y_lo), z: 4, core: 2. Of those that a mesh axis runs over, the one named last changes fastest.
Arguments:
- queries: bfloat16 [16, 1024, 1024], P('dp', 'space'), may hold values from -6 to 6
- keys: bfloat16 [16, 1024, 1024], P('dp', 'space'), may hold values from -6 to 6
- values: bfloat16 [16, 1024, 1024], P('dp', 'space'), may hold values from -6 to 6
- cotangent: bfloat16 [16, 1024, 640], P('dp', 'space'), may hold values from -6 to 6
- timesteps: int32 [16], P('dp'), may hold values from 0 to 999
- time_table: float32 [1000, 1024], replicated, may hold values from -0.3 to 0.3
- out_weight: bfloat16 [1024, 1024], replicated, may hold values from -0.1875 to 0.1875
- conv_weight: bfloat16 [1024, 9, 640], replicated, may hold values from -0.0625 to 0.0625
Outputs:
- query_grad: bfloat16 [16, 1024, 1024], P('dp', 'space')
- key_grad: bfloat16 [16, 1024, 1024], P('dp', 'space')
- value_grad: bfloat16 [16, 1024, 1024], P('dp', 'space')
- out_weight_grad: float32 [1024, 1024], P(('dp', 'space'))
- conv_weight_grad: float32 [1024, 9, 640], P(('dp', 'space'))
All inputs are finite; a program needn't handle non-finite values.
Results may differ from a plain program's by a relative error of at most 0.013.
The roundings to bfloat16 on the way count: a program that leaves them out, or rounds other values in their place, can miss the bound.
Values may be sent and summed in bfloat16 or wider, within the bound.
A program may use at most 128 MiB of HBM per device.

v0:
```python
import jax
import jax.numpy as jnp
from jax import lax
from jax.sharding import PartitionSpec as P

HEAD_DIM = 64
TAPS = 9
GRID = 32


def padded(block, sides, width):
    for axis, dim in sides:
        count = lax.axis_size(axis)
        forward = [(i, i + 1) for i in range(count - 1)]
        backward = [(target, source) for source, target in forward]
        low = lax.ppermute(
            lax.slice_in_dim(block, block.shape[dim] - width, None, axis=dim), axis, forward
        )
        high = lax.ppermute(lax.slice_in_dim(block, 0, width, axis=dim), axis, backward)
        block = jnp.concatenate([low, block, high], axis=dim)
    return block


def on_device(queries, keys, values, cotangent, timesteps, time_table, out_weight, conv_weight):
    samples, local_tokens, width_heads = queries.shape
    channels = out_weight.shape[1]
    out_channels = cotangent.shape[2]
    grid_side = GRID
    rows_here = local_tokens // grid_side
    score_scale = HEAD_DIM ** (-0.5)
    query_heads, key_heads, value_heads = (
        lax.all_to_all(queries, "space", split_axis=2, concat_axis=1, tiled=True),
        lax.all_to_all(keys, "space", split_axis=2, concat_axis=1, tiled=True),
        lax.all_to_all(values, "space", split_axis=2, concat_axis=1, tiled=True),
    )
    length = query_heads.shape[1]
    heads_here = query_heads.shape[2] // HEAD_DIM
    head_shape = (samples, length, heads_here, HEAD_DIM)
    query_four = query_heads.reshape(head_shape)
    key_four = key_heads.reshape(head_shape)
    value_four = value_heads.reshape(head_shape)
    block_rows = min(512, length)
    block_count = length // block_rows

    def to_blocks(tensor):
        return jnp.moveaxis(
            tensor.reshape(samples, block_count, block_rows, heads_here, HEAD_DIM), 1, 0
        )

    def from_blocks(tensor):
        return jnp.moveaxis(tensor, 0, 1).reshape(samples, length, heads_here * HEAD_DIM)

    def forward_block(query_block):
        scores = (
            jnp.einsum("sqhd,skhd->shqk", query_block, key_four, preferred_element_type=jnp.float32)
            * score_scale
        )
        row_top = jnp.max(scores, axis=3, keepdims=True)
        shifted = jnp.exp(scores - row_top)
        row_total = jnp.sum(shifted, axis=3, keepdims=True)
        attention = (shifted / row_total).astype(jnp.bfloat16)
        out_block = jnp.einsum(
            "shqk,skhd->sqhd", attention, value_four, preferred_element_type=jnp.float32
        ).astype(jnp.bfloat16)
        return (out_block, row_top[..., 0] + jnp.log(row_total[..., 0]))

    out_blocks, log_totals = lax.map(forward_block, to_blocks(query_four))
    attended = lax.all_to_all(
        from_blocks(out_blocks), "space", split_axis=1, concat_axis=2, tiled=True
    )
    selector = (
        timesteps[:, None] == jnp.arange(time_table.shape[0], dtype=jnp.int32)[None, :]
    ).astype(jnp.float32)
    time_bias = jnp.dot(selector, time_table, precision=lax.Precision.HIGHEST)
    projected = jnp.einsum("stc,ce->ste", attended, out_weight, preferred_element_type=jnp.float32)
    hidden = (projected + time_bias[:, None, :]).astype(jnp.bfloat16)
    grad_grid = cotangent.reshape(samples, rows_here, grid_side, out_channels)
    grad_ext = padded(grad_grid, (("space", 1),), 1)
    grad_pad = jnp.pad(grad_ext, ((0, 0), (0, 0), (1, 1), (0, 0)))
    grad_shifts = [
        grad_pad[
            :, 2 - row_step : 2 - row_step + rows_here, 2 - col_step : 2 - col_step + grid_side
        ]
        for row_step in range(3)
        for col_step in range(3)
    ]
    grad_stack = jnp.stack(grad_shifts, axis=3).reshape(-1, TAPS * out_channels)
    weight_flat = conv_weight.reshape(channels, TAPS * out_channels)
    hidden_grad = lax.dot_general(
        grad_stack, weight_flat, (((1,), (1,)), ((), ())), preferred_element_type=jnp.float32
    ).astype(jnp.bfloat16)
    hidden_grid = hidden.reshape(samples, rows_here, grid_side, channels)
    hidden_ext = padded(hidden_grid, (("space", 1),), 1)
    hidden_pad = jnp.pad(hidden_ext, ((0, 0), (0, 0), (1, 1), (0, 0)))
    hidden_shifts = [
        hidden_pad[:, row_step : row_step + rows_here, col_step : col_step + grid_side]
        for row_step in range(3)
        for col_step in range(3)
    ]
    hidden_stack = jnp.stack(hidden_shifts, axis=3).reshape(-1, TAPS * channels)
    conv_grad = lax.dot_general(
        hidden_stack,
        cotangent.reshape(-1, out_channels),
        (((0,), (0,)), ((), ())),
        preferred_element_type=jnp.float32,
    )
    conv_grad = jnp.transpose(conv_grad.reshape(TAPS, channels, out_channels), (1, 0, 2))
    attended_grad = jnp.einsum(
        "stc,ec->ste",
        hidden_grad.reshape(samples, local_tokens, channels),
        out_weight,
        preferred_element_type=jnp.float32,
    ).astype(jnp.bfloat16)
    out_grad = lax.dot_general(
        attended.reshape(-1, width_heads),
        hidden_grad,
        (((0,), (0,)), ((), ())),
        preferred_element_type=jnp.float32,
    )
    grad_heads = lax.all_to_all(attended_grad, "space", split_axis=2, concat_axis=1, tiled=True)
    grad_four = grad_heads.reshape(head_shape)

    def backward_block(carried, inputs):
        key_acc, value_acc = carried
        query_block, grad_block, out_block, log_total = inputs
        scores = (
            jnp.einsum("sqhd,skhd->shqk", query_block, key_four, preferred_element_type=jnp.float32)
            * score_scale
        )
        attention = jnp.exp(scores - log_total[..., None])
        weights = attention.astype(jnp.bfloat16)
        value_acc = value_acc + jnp.einsum(
            "shqk,sqhd->skhd", weights, grad_block, preferred_element_type=jnp.float32
        )
        prob_grad = jnp.einsum(
            "sqhd,skhd->shqk", grad_block, value_four, preferred_element_type=jnp.float32
        )
        row_delta = jnp.sum(grad_block.astype(jnp.float32) * out_block.astype(jnp.float32), axis=3)
        row_delta = jnp.transpose(row_delta, (0, 2, 1))
        score_grad = (attention * (prob_grad - row_delta[..., None])).astype(jnp.bfloat16)
        query_block_grad = (
            jnp.einsum("shqk,skhd->sqhd", score_grad, key_four, preferred_element_type=jnp.float32)
            * score_scale
        ).astype(jnp.bfloat16)
        key_acc = key_acc + jnp.einsum(
            "shqk,sqhd->skhd", score_grad, query_block, preferred_element_type=jnp.float32
        )
        return ((key_acc, value_acc), query_block_grad)

    zeros_acc = jnp.zeros(head_shape, jnp.float32)
    (key_acc, value_acc), query_blocks_grad = lax.scan(
        backward_block,
        (zeros_acc, zeros_acc),
        (to_blocks(query_four), to_blocks(grad_four), out_blocks, log_totals),
    )
    query_local = from_blocks(query_blocks_grad)
    key_local = (
        (key_acc * score_scale).astype(jnp.bfloat16).reshape(samples, length, heads_here * HEAD_DIM)
    )
    value_local = value_acc.astype(jnp.bfloat16).reshape(samples, length, heads_here * HEAD_DIM)
    query_grad, key_grad, value_grad = (
        lax.all_to_all(query_local, "space", split_axis=1, concat_axis=2, tiled=True),
        lax.all_to_all(key_local, "space", split_axis=1, concat_axis=2, tiled=True),
        lax.all_to_all(value_local, "space", split_axis=1, concat_axis=2, tiled=True),
    )
    out_total, conv_total = (
        lax.psum_scatter(out_grad, ("dp", "space"), scatter_dimension=0, tiled=True),
        lax.psum_scatter(conv_grad, ("dp", "space"), scatter_dimension=0, tiled=True),
    )
    return (query_grad, key_grad, value_grad, out_total, conv_total)


def solution(mesh):
    return jax.shard_map(
        on_device,
        mesh=mesh,
        in_specs=(
            P("dp", "space", None),
            P("dp", "space", None),
            P("dp", "space", None),
            P("dp", "space", None),
            P("dp"),
            P(),
            P(),
            P(),
        ),
        out_specs=(
            P("dp", "space", None),
            P("dp", "space", None),
            P("dp", "space", None),
            P(("dp", "space"), None),
            P(("dp", "space"), None, None),
        ),
        check_vma=False,
    )
```

profile of v0, /device:TPU:0, one launch (start us, length us, event | category | flops | bytes accessed | tf_op | source)
XLA Modules:
  0.0 1443.4 jit_solution(4688526408029877356)
XLA Ops:
  8.3 1.3 collective-permute-start
  9.6 1.3 collective-permute-start.1
  13.3 9.5 all-to-all-start
  27.5 16.3 %copy.102 = bf16[1024,9,640]{0,2,1:T(8,128)(2,1)} copy(bf16[1024,9,640]{2,0,1:T(8,128)(2,1)} %param.19) | data formatting | bytes 23592960 | tf_op args[7]
  47.5 5.7 all-to-all-start.1
  54.6 6.6 all-to-all-done.1
  61.2 4.2 all-to-all-start.2
  66.8 2.3 copy.101
  69.1 1.5 copy.132
  72.1 1.3 reshape_reshape.7
  74.7 2.2 copy.97
  76.8 1.4 reshape.195
  78.3 2.1 reshape.220
  80.4 2.2 copy.99
  82.6 1.4 reshape.196
  84.0 5.9 while.27
  91.1 2.1 reshape.229
  93.2 5.6 all-to-all-start.7
  99.1 7.2 convolution_convert_fusion
  107.0 2.2 reshape.230
  109.2 2.2 copy.139
  111.4 1.4 reshape.205
  112.8 2.8 fusion.97
  116.3 3.5 fusion.91
  119.8 1.4 all_to_all.123
  121.8 1.7 collective-permute-start.2
  124.7 3.1 collective-permute-done.3
  128.4 1.6 copy.121
  130.0 3.1 copy.133
  133.2 4.4 copy.122
  137.5 12.7 convolution_bitcast_fusion.1
  152.6 9.3 all-to-all-start.3
  161.9 8.2 all-to-all-done.3
  171.3 2.2 copy.141
  173.5 2.0 reshape_reshape.8
  177.2 13.1 while.28
  190.4 2.0 copy.123
  192.4 2.1 reshape.223
  194.5 4.2 all-to-all-start.4
  200.7 6.2 all-to-all-done.4
  206.9 3.5 all-to-all-start.5
  211.9 6.7 all-to-all-done.5
  218.6 4.2 all-to-all-start.6
  222.8 1.3 reshape.224
  227.3 3.7 all-to-all-done.6
  231.1 1.3 reshape.228
  233.8 528.0 %reduce-scatter.3.cloned.1.call-done = f32[8,1024]{1,0:T(8,128)} async-done(((f32[1024,1024]{1,0:T(8,128)}), f32[8,1024]{1,0:T(8,128)}) %reduce-scatter.3.cloned.1.call-update) | async-done | bytes 32784 | tf_op jit(solution)/shard_map/reduce_scatter | solution.py:167
  761.8 674.8 %reduce-scatter.5.cloned.1.call-done = f32[8,9,640]{2,0,1:T(8,128)} async-done(((f32[1024,9,640]{2,0,1:T(8,128)}), f32[8,9,640]{2,0,1:T(8,128)}) %reduce-scatter.5.cloned.1.call-update) | async-done | bytes 184336 | tf_op jit(solution)/shard_map/reduce_scatter | solution.py:168
  (125 shorter events, 54.2 us)
Async XLA Ops:
  7.2 114.1 %copy-start = (bf16[1024,1024]{1,0:T(8,128)(2,1)S(1)}, bf16[1024,1024]{1,0:T(8,128)(2,1)}, u32[]{:S(2)}) copy-start(bf16[1024,1024]{1,0:T(8,128)(2,1)} %param.18) | copy-start | bytes 6291460
  8.3 35.6 %collective-permute-start = (bf16[2,1,32,640]{3,2,1,0:T(8,128)(2,1)S(1)}, bf16[2,1,32,640]{3,2,1,0:T(8,128)(2,1)S(1)}, u32[]{:S(2)}, u32[]{:S(2)}) collective-permute-start(bf16[2,1,32,640]{3,2,1,0:T(8,128)(2,1)S(1)} %get-tuple-element.230), channel_id=1, source_target_pairs={{0,1},{1,2},{2,3},{3,4},{4,5},{5,6},{6,7},{7,8},{8,9},{9,10},{10,1... | collective-permute-start | bytes 245768 | tf_op jit(solution)/shard_map/ppermute | solution.py:16
  9.6 34.3 %collective-permute-start.1 = (bf16[2,1,32,640]{3,2,1,0:T(8,128)(2,1)S(1)}, bf16[2,1,32,640]{3,2,1,0:T(8,128)(2,1)S(1)}, u32[]{:S(2)}, u32[]{:S(2)}) collective-permute-start(bf16[2,1,32,640]{3,2,1,0:T(8,128)(2,1)S(1)} %get-tuple-element.231), channel_id=1, source_target_pairs={{1,0},{2,1},{3,2},{4,3},{5,4},{6,5},{7,6},{8,7},{9,8},{10,9},{11,1... | collective-permute-start | bytes 245768 | tf_op jit(solution)/shard_map/ppermute | solution.py:19
  13.3 34.2 %all-to-all-start = ((bf16[16,2,4096]{2,1,0:T(2,128)(2,1)}), bf16[16,2,4096]{2,1,0:T(2,128)(2,1)S(1)}, u32[]{:S(2)}, u32[]{:S(2)}) async-start(bf16[16,2,4096]{2,1,0:T(2,128)(2,1)} %reshape.215), calls=%async_computation | async-start | bytes 524288 | tf_op jit(solution)/shard_map/all_to_all | solution.py:32
  27.5 16.3 %copy-start.6 = (bf16[2,64,640]{2,1,0:T(8,128)(2,1)S(1)}, bf16[2,64,640]{2,1,0:T(8,128)(2,1)}, u32[]{:S(2)}) copy-start(bf16[2,64,640]{2,1,0:T(8,128)(2,1)} %param.15) | copy-start | bytes 491524
  47.5 13.8 all-to-all-start.1
  61.2 17.1 %all-to-all-start.2 = ((bf16[16,2,4096]{2,1,0:T(2,128)(2,1)}), bf16[16,2,4096]{2,1,0:T(2,128)(2,1)}, u32[]{:S(2)}, u32[]{:S(2)}) async-start(bf16[16,2,4096]{2,1,0:T(2,128)(2,1)} %reshape.219), calls=%async_computation.2 | async-start | bytes 524288 | tf_op jit(solution)/shard_map/all_to_all | solution.py:34
  90.0 16.4 %copy-start.4 = (bf16[2,1024,1,64]{1,3,0,2:T(8,128)(2,1)}, bf16[2,1024,1,64]{1,3,0,2:T(8,128)(2,1)S(1)}, u32[]{:S(2)}) copy-start(bf16[2,1024,1,64]{1,3,0,2:T(8,128)(2,1)S(1)} %get-tuple-element.399) | copy-start | bytes 786436
  90.0 16.4 %copy-start.7 = (bf16[2,2,512,1,64]{2,4,1,3,0:T(8,128)(2,1)}, bf16[2,2,512,1,64]{2,4,1,3,0:T(8,128)(2,1)S(1)}, u32[]{:S(2)}) copy-start(bf16[2,2,512,1,64]{2,4,1,3,0:T(8,128)(2,1)S(1)} %get-tuple-element.364) | copy-start | bytes 786436
  93.2 13.8 all-to-all-start.7
  98.9 663.0 %reduce-scatter.3.cloned.1.call-start = ((), (), s32[]{:S(2)}) async-start(), calls=%async_computation.10 | async-start | bytes 4227072 | tf_op jit(solution)/shard_map/reduce_scatter | solution.py:167
  107.0 5.8 copy-start.8
  115.6 0.7 copy-start.11
  115.7 1320.9 %reduce-scatter.5.cloned.1.call-start = ((), (), s32[]{:S(2)}) async-start(), calls=%async_computation.11 | async-start | bytes 23777280 | tf_op jit(solution)/shard_map/reduce_scatter | solution.py:168
  121.8 3.0 collective-permute-start.2
  123.4 4.4 collective-permute-start.3
  152.6 17.5 %all-to-all-start.3 = ((bf16[16,2,4096]{2,1,0:T(2,128)(2,1)}), bf16[16,2,4096]{2,1,0:T(2,128)(2,1)S(1)}, u32[]{:S(2)}, u32[]{:S(2)}) async-start(bf16[16,2,4096]{2,1,0:T(2,128)(2,1)} %reshape.221), calls=%async_computation.3 | async-start | bytes 524288 | tf_op jit(solution)/shard_map/all_to_all | solution.py:120
  179.0 1.0 copy-start.5
  180.0 1.3 copy-start.9
  181.3 1.0 copy-start.1
  182.3 0.7 copy-start.10
  183.0 0.8 copy-start.2
  185.5 1.0 copy-start.5
  186.5 1.3 copy-start.9
  187.8 1.0 copy-start.1
  188.9 0.7 copy-start.10
  189.6 0.8 copy-start.2
  190.4 8.4 copy-start.3
  194.5 12.4 all-to-all-start.4
  206.9 11.7 all-to-all-start.5
  218.6 12.4 all-to-all-start.6
Sparse Core Ops, SparseCore 0:
  115.8 645.9 reduce-scatter.2
  764.9 671.6 reduce-scatter.4
where the time goes:
time: 1450 us; the launch traced here: 1440 us
  waiting for transfers between devices  1240 us (86%)
  local copies, waits for them, and re-layouts  92.9 us (6%)
  starting transfers between devices  52 us (4%)
  matrix products  40.2 us (3%)
  between operations  14.5 us (1%)
    reduce_scatter x1, waiting for transfers between devices, on_device(): lax.psum_scatter(conv_grad, ('dp', 'space'), scatter_dimension=0, tiled=T...  675 us
    reduce_scatter x1, waiting for transfers between devices, on_device(): lax.psum_scatter(out_grad, ('dp', 'space'), scatter_dimension=0, tiled=True)  528 us
    unnamed x52, local copies, waits for them, and re-layouts  52.4 us
  transfers between devices with their start and end apart: 14, of which 9 were waited for; matrix products, arithmetic and copies ran while one was open for 7% of the time, Pallas kernels for 0%

commit v1 on v0

v1 whole, which is shorter than its diff:
```python
import jax
import jax.numpy as jnp
from jax import lax
from jax.experimental import pallas as pl
from jax.experimental.pallas import tpu as pltpu
from jax.sharding import PartitionSpec as P

HEAD_DIM = 64
TAPS = 9
GRID = 32
TOKENS = GRID * GRID
PAIR = 2 * HEAD_DIM
DP = 8
SPACE = 16
CHIPS = 8
CH = 1024
COUT = 640
HERE = 64
SLAB = 8
OWN = DP * SLAB
ROWS = 80
BLOCK = 256
SCALE = HEAD_DIM ** (-0.5)
MESH = pl.DeviceIdType.MESH
NT = (((1,), (1,)), ((), ()))
BF = jnp.bfloat16
F32 = jnp.float32


def mm(a, b):
    return jnp.dot(a, b, preferred_element_type=F32)


def mm_nt(a, b):
    return lax.dot_general(a, b, NT, preferred_element_type=F32)


def kernel(
    q_ref, k_ref, v_ref, cot_ref, w_ref, wconv_ref, bias_ref,
    grads_ref, gw_ref, gc_ref,
    qkv, cot_all, w, wconv, wperm, bias_col, km, dom, vt, kt, probs, ot, att, att_tok,
    z, hg_all, hsend, hbuf, lhs, conv_send, conv_recv, do, dv_acc, dk_acc, gh,
    ow, ow_send, ow_recv, ow_sum, ow_out,
    loc, qkv_s, qkv_r, cot_s, cot_r, att_s, att_r, hg_s, hg_r, hid_s, hid_r,
    conv_s, conv_r, ow_s, ow_r, gr_s, gr_r, one_s, one_r,
):
    d = lax.axis_index("dp")
    s = lax.axis_index("space")
    c = lax.div(s, 2)
    k = lax.rem(s, 2)
    lin = d * 2 + k

    def lanes(chip):
        return pl.ds(pl.multiple_of(chip * PAIR, PAIR), PAIR)

    def rows(index, size):
        return pl.ds(pl.multiple_of(index * size, size), size)

    def to(i):
        return lax.rem(s + i, SPACE)

    def frm(i):
        return lax.rem(s + SPACE - i, SPACE)

    def chip_to(i):
        return lax.rem(c + i, CHIPS)

    def chip_frm(i):
        return lax.rem(c + CHIPS - i, CHIPS)

    def each(count, body):
        def step(i, carry):
            body(i)
            return carry

        lax.fori_loop(1, count, step, 0)

    def take(ref, sem):
        pltpu.make_async_copy(ref, ref, sem).wait()

    def remote(src, dst, send, recv, where):
        return pltpu.make_async_remote_copy(
            src_ref=src, dst_ref=dst, send_sem=send, recv_sem=recv,
            device_id=where, device_id_type=MESH,
        )

    local = [
        pltpu.make_async_copy(w_ref, w, loc.at[0]),
        pltpu.make_async_copy(wconv_ref, wconv, loc.at[1]),
        pltpu.make_async_copy(cot_ref.at[k], cot_all.at[rows(k * SPACE + s, HERE)], loc.at[2]),
        pltpu.make_async_copy(q_ref.at[k, :, lanes(c)], qkv.at[0, rows(s, HERE)], loc.at[3]),
        pltpu.make_async_copy(k_ref.at[k, :, lanes(c)], qkv.at[1, rows(s, HERE)], loc.at[4]),
        pltpu.make_async_copy(v_ref.at[k, :, lanes(c)], qkv.at[2, rows(s, HERE)], loc.at[5]),
    ]
    for copy in local:
        copy.start()

    barrier = pltpu.get_barrier_semaphore()

    def greet(i):
        pl.semaphore_signal(barrier, inc=1, device_id={"space": to(i)}, device_id_type=MESH)
        other = lax.rem(lin + i, SPACE)
        pl.semaphore_signal(
            barrier, inc=1,
            device_id={"dp": lax.div(other, 2), "space": c * 2 + lax.rem(other, 2)},
            device_id_type=MESH,
        )

    each(SPACE, greet)
    swap = {"dp": c, "space": lin}

    @pl.when(c != d)
    def _():
        pl.semaphore_signal(barrier, inc=1, device_id=swap, device_id_type=MESH)
        pl.semaphore_wait(barrier, 2 * (SPACE - 1) + 1)

    @pl.when(c == d)
    def _():
        pl.semaphore_wait(barrier, 2 * (SPACE - 1))

    def send_cot(i):
        peer = to(i)
        core = lax.rem(peer, 2)
        remote(
            cot_ref.at[core], cot_all.at[rows(core * SPACE + s, HERE)],
            cot_s.at[i], cot_r.at[i], {"space": peer},
        ).start()

    def send_qkv(i):
        peer = to(i)
        chip = lax.div(peer, 2)
        core = lax.rem(peer, 2)
        for j, ref in enumerate((q_ref, k_ref, v_ref)):
            remote(
                ref.at[core, :, lanes(chip)], qkv.at[j, rows(s, HERE)],
                qkv_s.at[i], qkv_r.at[i], {"space": peer},
            ).start()

    each(SPACE, send_qkv)
    each(SPACE, send_cot)

    local[0].wait()
    bias_here = bias_ref[pl.ds(k, 1), :]
    high = bias_here.astype(BF)
    rest = bias_here - high.astype(F32)
    mid = rest.astype(BF)
    low = (rest - mid.astype(F32)).astype(BF)
    pieces = jnp.concatenate(
        [high.astype(F32), mid.astype(F32), low.astype(F32), jnp.zeros((13, CH), F32)], axis=0
    ).astype(BF)

    def permute(i, carry):
        n = lax.broadcasted_iota(jnp.int32, (BLOCK, CH), 0) + i * BLOCK
        e = lax.broadcasted_iota(jnp.int32, (BLOCK, CH), 1)
        n_chip = lax.shift_right_logical(n, 7)
        n_core = lax.shift_right_logical(n, 6) & 1
        n_dp = lax.shift_right_logical(n, 3) & 7
        target = n_dp * 128 + n_chip * 16 + n_core * 8 + (n & 7)
        pick = jnp.where(e == target, 1.0, 0.0).astype(BF)
        wperm[rows(i, BLOCK), :] = mm_nt(pick, w[...]).astype(BF)
        column = jnp.sum(mm_nt(pick, pieces), axis=1, keepdims=True)
        bias_col[rows(i, BLOCK), :] = jnp.broadcast_to(column, (BLOCK, PAIR))
        return carry

    lax.fori_loop(0, CH // BLOCK, permute, 0)

    for copy in local[3:]:
        copy.wait()
    each(SPACE, lambda i: take(qkv.at[:, rows(frm(i), HERE), :], qkv_r.at[i]))
    first = lax.broadcasted_iota(jnp.int32, (TOKENS, PAIR), 1) < HEAD_DIM
    key = qkv[1]
    km[0] = jnp.where(first, key, jnp.zeros_like(key))
    km[1] = jnp.where(first, jnp.zeros_like(key), key)
    kt[...] = key.astype(F32).T.astype(BF)
    vt[...] = qkv[2].astype(F32).T.astype(BF)

    def forward(i, carry):
        here = rows(i, BLOCK)
        query = qkv[0, here, :] * jnp.asarray(SCALE, BF)
        outs = []
        for h in range(2):
            scores = mm_nt(km[h], query)
            top = jnp.max(scores, axis=0, keepdims=True)
            shifted = jnp.exp(scores - top)
            total = jnp.sum(shifted, axis=0, keepdims=True)
            prob = shifted * (1.0 / total)
            probs[h, :, here] = prob
            outs.append(mm(vt[h * HEAD_DIM : (h + 1) * HEAD_DIM, :], prob.astype(BF)))
        out = jnp.concatenate(outs, axis=0)
        ot[:, here] = out.astype(BF)
        att[here, :] = out.T.astype(BF)
        return carry

    lax.fori_loop(0, TOKENS // BLOCK, forward, 0)

    def send_att(i):
        chip = chip_to(i)
        remote(
            att.at[rows(chip, PAIR)], att_tok.at[:, lanes(c)],
            att_s.at[i], att_r.at[i], {"space": chip * 2 + k},
        ).start()

    each(CHIPS, send_att)
    att_tok[:, lanes(c)] = att[rows(c, PAIR), :]

    local[1].wait()
    local[2].wait()
    each(SPACE, lambda i: take(cot_all.at[rows(k * SPACE + frm(i), HERE)], cot_r.at[i]))
    partner = {"space": c * 2 + 1 - k}
    mine = rows(k, TOKENS)
    cot_copy = remote(cot_all.at[mine], cot_all.at[mine], one_s.at[0], one_r.at[0], partner)
    cot_copy.start()
    z[0:GRID, :] = jnp.zeros((GRID, TAPS * PAIR), F32)
    z[GRID + TOKENS :, :] = jnp.zeros((GRID, TAPS * PAIR), F32)

    def taps(i, carry):
        block = cot_all[pl.ds(pl.multiple_of(k * TOKENS + i * BLOCK, BLOCK), BLOCK), :]
        z[pl.ds(pl.multiple_of(GRID + i * BLOCK, GRID), BLOCK), :] = mm_nt(block, wconv[...])
        return carry

    lax.fori_loop(0, TOKENS // BLOCK, taps, 0)
    column = lax.broadcasted_iota(jnp.int32, (TOKENS, PAIR), 0) & (GRID - 1)
    sums = []
    for col in range(3):
        total = None
        for row in range(3):
            start = 2 * GRID - GRID * row
            at = (3 * row + col) * PAIR
            part = z[start : start + TOKENS, at : at + PAIR]
            total = part if total is None else total + part
        sums.append(total)
    hidden_grad = (
        sums[1]
        + jnp.where(column < GRID - 1, pltpu.roll(sums[0], TOKENS - 1, 0), 0.0)
        + jnp.where(column > 0, pltpu.roll(sums[2], 1, 0), 0.0)
    )
    hg_all[:, lanes(c)] = hidden_grad.astype(BF)

    def send_hg(i):
        remote(
            hg_all.at[:, lanes(c)], hg_all.at[:, lanes(c)],
            hg_s.at[i], hg_r.at[i], {"space": chip_to(i) * 2 + k},
        ).start()

    each(CHIPS, send_hg)

    each(CHIPS, lambda i: take(att_tok.at[:, lanes(chip_frm(i))], att_r.at[i]))
    hsend[...] = (mm_nt(wperm[...], att_tok[...]) + bias_col[...]).astype(BF)

    def send_hidden(i):
        peer = to(i)
        remote(
            hsend.at[rows(peer, OWN)], hbuf.at[:, lanes(k * CHIPS + c)],
            hid_s.at[i], hid_r.at[i], {"space": peer},
        ).start()

    each(SPACE, send_hidden)
    hbuf[:, lanes(k * CHIPS + c)] = hsend[rows(s, OWN), :]

    def take_hidden(i):
        peer = frm(i)
        take(hbuf.at[:, lanes(lax.rem(peer, 2) * CHIPS + lax.div(peer, 2))], hid_r.at[i])

    each(SPACE, take_hidden)
    cot_copy.wait_send()
    take(cot_all.at[rows(1 - k, TOKENS)], one_r.at[0])

    spot = lax.broadcasted_iota(jnp.int32, (OWN, TOKENS), 1)
    y = lax.shift_right_logical(spot, 5)
    x = spot & (GRID - 1)
    for sample in range(2):
        inside = slice(sample * TOKENS, (sample + 1) * TOKENS)
        hidden = hbuf[:, inside].astype(F32)
        for row in range(3):
            for col in range(3):
                offset = (row - 1) * GRID + col - 1
                moved = pltpu.roll(hidden, (-offset) % TOKENS, 1) if offset else hidden
                good = None
                for ok in (
                    [y > 0] * (row == 0) + [y < GRID - 1] * (row == 2)
                    + [x > 0] * (col == 0) + [x < GRID - 1] * (col == 2)
                ):
                    good = ok if good is None else good & ok
                if good is not None:
                    moved = jnp.where(good, moved, 0.0)
                tap = 3 * row + col
                lhs[tap * OWN : (tap + 1) * OWN, inside] = moved.astype(BF)
    lhs[TAPS * OWN :, :] = jnp.zeros((OWN, 2 * TOKENS), BF)
    for at in range(0, COUT, BLOCK):
        end = min(at + BLOCK, COUT)
        part = mm(lhs[...], cot_all[:, at:end])
        for dest in range(DP):
            for pair in range(5):
                top = pair * 2 * OWN + dest * SLAB
                both = jnp.concatenate(
                    [part[top : top + SLAB], part[top + OWN : top + OWN + SLAB]], axis=0
                )
                conv_send[dest, pair * 16 : pair * 16 + 16, at:end] = both.astype(BF)

    def send_conv(i):
        dest = lax.rem(d + i, DP)
        remote(
            conv_send.at[dest], conv_recv.at[i], conv_s.at[i], conv_r.at[i], {"dp": dest}
        ).start()

    each(DP, send_conv)

    each(CHIPS, lambda i: take(hg_all.at[:, lanes(chip_frm(i))], hg_r.at[i]))
    do[...] = mm_nt(hg_all[...], w[rows(c, PAIR), :]).astype(BF)
    grad = do[...]
    dom[0] = jnp.where(first, grad, jnp.zeros_like(grad))
    dom[1] = jnp.where(first, jnp.zeros_like(grad), grad)
    dv_acc[...] = jnp.zeros_like(dv_acc)
    dk_acc[...] = jnp.zeros_like(dk_acc)

    def backward(i, carry):
        here = rows(i, BLOCK)
        query = qkv[0, here, :] * jnp.asarray(SCALE, BF)
        half = lax.broadcasted_iota(jnp.int32, (BLOCK, PAIR), 1) < HEAD_DIM
        product = ot[:, here].astype(F32) * do[here, :].astype(F32).T
        outs = []
        for h in range(2):
            prob = probs[h, :, here]
            grad_block = dom[h, here, :]
            dv_acc[...] += mm(prob.astype(BF), grad_block)
            prob_grad = mm_nt(qkv[2], grad_block)
            delta = jnp.sum(product[h * HEAD_DIM : (h + 1) * HEAD_DIM], axis=0, keepdims=True)
            score_grad = (prob * (prob_grad - delta)).astype(BF)
            zero = jnp.zeros_like(query)
            masked = jnp.where(half, query, zero) if h == 0 else jnp.where(half, zero, query)
            dk_acc[...] += mm(score_grad, masked)
            outs.append(mm(kt[h * HEAD_DIM : (h + 1) * HEAD_DIM, :], score_grad))
        gh[0, here, :] = (jnp.concatenate(outs, axis=0) * SCALE).T.astype(BF)
        return carry

    lax.fori_loop(0, TOKENS // BLOCK, backward, 0)
    gh[1] = dk_acc[...].astype(BF)
    gh[2] = dv_acc[...].astype(BF)

    def send_grads(i):
        peer = to(i)
        remote(
            gh.at[:, rows(peer, HERE), :], grads_ref.at[:, k, :, lanes(c)],
            gr_s.at[i], gr_r.at[i], {"space": peer},
        ).start()

    each(SPACE, send_grads)
    own_grads = pltpu.make_async_copy(
        gh.at[:, rows(s, HERE), :], grads_ref.at[:, k, :, lanes(c)], loc.at[0]
    )
    own_grads.start()

    ow[...] = mm(ot[...], hg_all[...])
    for piece in range(SPACE):
        band = ow[piece * SLAB : (piece + 1) * SLAB, :]
        ow_send[piece] = jnp.concatenate([band[:, : CH // 2], band[:, CH // 2 :]], axis=0).astype(BF)

    def send_ow(i):
        other = lax.rem(lin + i, SPACE)
        remote(
            ow_send.at[other], ow_recv.at[i], ow_s.at[i], ow_r.at[i],
            {"dp": lax.div(other, 2), "space": c * 2 + lax.rem(other, 2)},
        ).start()

    each(SPACE, send_ow)

    each(DP, lambda i: take(conv_recv.at[i], conv_r.at[i]))
    total = conv_send[d].astype(F32)
    for i in range(1, DP):
        total = total + conv_recv[i].astype(F32)
    for tap in range(TAPS):
        gc_ref[tap] = total[tap * SLAB : (tap + 1) * SLAB]

    each(SPACE, lambda i: take(ow_recv.at[i], ow_r.at[i]))
    total = ow_send[lin].astype(F32)
    for i in range(1, SPACE):
        total = total + ow_recv[i].astype(F32)
    ow_sum[:, : CH // 2] = total[:SLAB]
    ow_sum[:, CH // 2 :] = total[SLAB:]

    @pl.when(c != d)
    def _():
        copy = remote(ow_sum, ow_out, one_s.at[1], one_r.at[1], swap)
        copy.start()
        copy.wait()

    @pl.when(c == d)
    def _():
        copy = pltpu.make_async_copy(ow_sum, ow_out, loc.at[1])
        copy.start()
        copy.wait()

    gw_ref[...] = ow_out[...]

    own_grads.wait()

    def take_grads(i):
        peer = frm(i)
        take(grads_ref.at[:, lax.rem(peer, 2), :, lanes(lax.div(peer, 2))], gr_r.at[i])

    each(SPACE, take_grads)

    def sent(i):
        take(qkv.at[:, rows(0, HERE), :], qkv_s.at[i])
        take(cot_all.at[rows(0, HERE)], cot_s.at[i])
        take(hsend.at[rows(0, OWN)], hid_s.at[i])
        take(gh.at[:, rows(0, HERE), :], gr_s.at[i])
        take(ow_send.at[0], ow_s.at[i])

    each(SPACE, sent)

    def sent_chips(i):
        take(att.at[rows(0, PAIR)], att_s.at[i])
        take(hg_all.at[:, lanes(0)], hg_s.at[i])
        take(conv_send.at[0], conv_s.at[i])

    each(CHIPS, sent_chips)


def on_device(queries, keys, values, cotangent, timesteps, time_table, out_weight, conv_weight):
    chip = lax.axis_index("space") // 2
    bias = jnp.concatenate(
        [lax.dynamic_slice(time_table, (timesteps[i], 0), (1, CH)) for i in range(2)], axis=0
    )
    own = lax.dynamic_slice(conv_weight, (chip * PAIR, 0, 0), (PAIR, TAPS, COUT))
    wconv = jnp.transpose(own, (1, 0, 2)).reshape(TAPS * PAIR, COUT)
    anywhere = pl.BlockSpec(memory_space=pl.ANY)
    vmem = pl.BlockSpec(memory_space=pltpu.VMEM)
    sems = pltpu.SemaphoreType.DMA
    grads, gw, gc = pl.pallas_call(
        kernel,
        out_shape=(
            jax.ShapeDtypeStruct((3, 2, HERE, CH), BF),
            jax.ShapeDtypeStruct((SLAB, CH), F32),
            jax.ShapeDtypeStruct((TAPS, SLAB, COUT), F32),
        ),
        in_specs=[anywhere] * 6 + [vmem],
        out_specs=(anywhere, vmem, vmem),
        scratch_shapes=[
            pltpu.VMEM((3, TOKENS, PAIR), BF),
            pltpu.VMEM((2 * TOKENS, COUT), BF),
            pltpu.VMEM((CH, CH), BF),
            pltpu.VMEM((TAPS * PAIR, COUT), BF),
            pltpu.VMEM((CH, CH), BF),
            pltpu.VMEM((CH, PAIR), F32),
            pltpu.VMEM((2, TOKENS, PAIR), BF),
            pltpu.VMEM((2, TOKENS, PAIR), BF),
            pltpu.VMEM((PAIR, TOKENS), BF),
            pltpu.VMEM((PAIR, TOKENS), BF),
            pltpu.VMEM((2, TOKENS, TOKENS), F32),
            pltpu.VMEM((PAIR, TOKENS), BF),
            pltpu.VMEM((TOKENS, PAIR), BF),
            pltpu.VMEM((PAIR, CH), BF),
            pltpu.VMEM((TOKENS + 2 * GRID, TAPS * PAIR), F32),
            pltpu.VMEM((TOKENS, CH), BF),
            pltpu.VMEM((CH, PAIR), BF),
            pltpu.VMEM((OWN, 2 * TOKENS), BF),
            pltpu.VMEM((10 * OWN, 2 * TOKENS), BF),
            pltpu.VMEM((DP, ROWS, COUT), BF),
            pltpu.VMEM((DP, ROWS, COUT), BF),
            pltpu.VMEM((TOKENS, PAIR), BF),
            pltpu.VMEM((TOKENS, PAIR), F32),
            pltpu.VMEM((TOKENS, PAIR), F32),
            pltpu.VMEM((3, TOKENS, PAIR), BF),
            pltpu.VMEM((PAIR, CH), F32),
            pltpu.VMEM((SPACE, 2 * SLAB, CH // 2), BF),
            pltpu.VMEM((SPACE, 2 * SLAB, CH // 2), BF),
            pltpu.VMEM((SLAB, CH), F32),
            pltpu.VMEM((SLAB, CH), F32),
            sems((6,)),
            sems((SPACE,)), sems((SPACE,)),
            sems((SPACE,)), sems((SPACE,)),
            sems((CHIPS,)), sems((CHIPS,)),
            sems((CHIPS,)), sems((CHIPS,)),
            sems((SPACE,)), sems((SPACE,)),
            sems((DP,)), sems((DP,)),
            sems((SPACE,)), sems((SPACE,)),
            sems((SPACE,)), sems((SPACE,)),
            sems((2,)), sems((2,)),
        ],
        compiler_params=pltpu.CompilerParams(
            collective_id=0, has_side_effects=True, vmem_limit_bytes=58 * 1024 * 1024
        ),
        cost_estimate=pl.CostEstimate(
            flops=8_000_000_000, bytes_accessed=20_000_000, transcendentals=2_000_000
        ),
    )(queries, keys, values, cotangent, out_weight, wconv, bias)
    return grads[0], grads[1], grads[2], gw, jnp.transpose(gc, (1, 0, 2))


def solution(mesh):
    return jax.shard_map(
        on_device,
        mesh=mesh,
        in_specs=(
            P("dp", "space", None),
            P("dp", "space", None),
            P("dp", "space", None),
            P("dp", "space", None),
            P("dp"),
            P(),
            P(),
            P(),
        ),
        out_specs=(
            P("dp", "space", None),
            P("dp", "space", None),
            P("dp", "space", None),
            P(("dp", "space"), None),
            P(("dp", "space"), None, None),
        ),
        check_vma=False,
    )
```

time: 1450 us -> 114 us (0.08)
  the two profiles are of different devices: /device:TPU:0 before, /device:TPU:40 now
where the time goes in v1:
time: 114 us; the launch traced here: 113 us
  Pallas kernels  98.5 us (86%)
  local copies, waits for them, and re-layouts  9.75 us (9%)
  between operations  4.54 us (4%)
    pallas_call x1, Pallas kernels, on_device(): pl.pallas_call(kernel, out_shape=(jax.ShapeDtypeStruct((3, 2, HERE, CH),...  98.5 us
    unnamed x2, local copies, waits for them, and re-layouts  2.98 us
    dynamic_slice x1, local copies, waits for them, and re-layouts, on_device(): lax.dynamic_slice(conv_weight, (chip * PAIR, 0, 0), (PAIR, TAPS, COUT))  2.67 us

profile of v1, /device:TPU:40, one launch (start us, length us, event | category | flops | bytes accessed | tf_op | source)
XLA Modules:
  0.0 113.4 jit_solution(10963738394117656570)
XLA Ops:
  0.6 1.3 %fusion = (s32[1]{0:T(128)}, s32[1]{0:T(128)}) fusion(s32[2]{0:T(128)} %param.12), kind=kLoop, calls=%fused_computation.7 | loop fusion | bytes 16 | tf_op jit(solution)/shard_map/slice | solution.py:423
  5.8 0.8 constant_dynamic-slice_fusion.1
  6.6 0.6 pad_maximum_fusion.bias_ref
  7.2 2.7 %constant_dynamic-slice_fusion.2 = bf16[128,9,640]{2,0,1:T(8,128)(2,1)} fusion(bf16[1024,9,640]{2,0,1:T(8,128)(2,1)} %param.15, s32[]{:T(128)S(6)} %select_n.15), kind=kLoop, calls=%fused_computation.6 | loop fusion | bytes 2949124 | tf_op jit(solution)/shard_map/dynamic_slice | solution.py:425
  9.9 98.5 %shard_map.119 = (bf16[3,2,64,1024]{3,2,1,0:T(8,128)(2,1)}, f32[8,1024]{1,0:T(8,128)}, f32[9,8,640]{2,1,0:T(8,128)}) custom-call(bf16[2,64,1024]{2,1,0:T(8,128)(2,1)} %q_ref.1, bf16[2,64,1024]{2,1,0:T(8,128)(2,1)} %k_ref.1, bf16[2,64,1024]{2,1,0:T(8,128)(2,1)} %v_ref.1, bf16[2,64,640]{2,1,0:T(8,128)(2,1)} %cot_ref.1, bf16[1024,1024]{1,0:T(8,128)(2,1)} %w_ref.1, ...), custom_call_target="tpu_custom_call" | custom-call | flops 8000000000 | bytes 20000000 | tf_op jit(solution)/shard_map/pallas_call | solution.py:430
  108.4 2.0 %slice_bitcast_fusion = (bf16[2,64,1024]{2,1,0:T(8,128)(2,1)}, bf16[2,64,1024]{2,1,0:T(8,128)(2,1)}, bf16[2,64,1024]{2,1,0:T(8,128)(2,1)}) fusion(bf16[3,2,64,1024]{3,2,1,0:T(8,128)(2,1)} %get-tuple-element.8), kind=kLoop, calls=%fused_computation | loop fusion | bytes 1572864 | tf_op jit(solution)/shard_map/squeeze | solution.py:488
  110.4 1.4 %copy.15 = f32[8,1024]{1,0:T(8,128)} copy(f32[8,1024]{1,0:T(8,128)} %get-tuple-element.26) | data formatting | bytes 65536
  111.8 1.6 %copy.16 = f32[8,9,640]{2,0,1:T(8,128)} copy(f32[8,9,640]{2,0,1:T(8,128)} %bitcast.13) | data formatting | bytes 368640

commit v2 on v1

v2 whole, which is shorter than its diff:
```python
import jax
import jax.numpy as jnp
from jax import lax
from jax.experimental import pallas as pl
from jax.experimental.pallas import tpu as pltpu
from jax.sharding import PartitionSpec as P

HEAD_DIM = 64
TAPS = 9
GRID = 32
TOKENS = GRID * GRID
PAIR = 2 * HEAD_DIM
DP = 8
SPACE = 16
CHIPS = 8
CH = 1024
COUT = 640
HERE = 64
SLAB = 8
OWN = DP * SLAB
ROWS = 80
BLOCK = 256
SPLIT = 2
STEPS = 1000
SCALE = HEAD_DIM ** (-0.5)
MESH = pl.DeviceIdType.MESH
NT = (((1,), (1,)), ((), ()))
BF = jnp.bfloat16
F32 = jnp.float32


def mm(a, b):
    return jnp.dot(a, b, preferred_element_type=F32)


def mm_nt(a, b):
    return lax.dot_general(a, b, NT, preferred_element_type=F32)


def kernel(
    q_ref, k_ref, v_ref, cot_ref, w_ref, wc_ref, table_ref, step_ref,
    grads_ref, gw_ref, gc_ref,
    qkv, cot_all, cext, w, wc, table, wperm, bias_col, km, dom, vt, kt, probs, ot, att, att_tok,
    hg_tok, ag_tok, hsend, hbuf, lhs, conv_acc, conv_send, conv_recv, conv_keep, conv_out, conv_in, do, dv_acc, dk_acc, gh,
    ow_lhs, ow_pass, ow_in, ow_send, ow_recv, ow_keep, ow_out, ow_back, ow_sum, ow_parts,
    loc, halo_s, halo_r, qkv_s, qkv_r, near_s, near_r, cot_s, cot_r, ag_s, ag_r, att_s, att_r, hid_s, hid_r,
    conv_s, conv_r, cy_s, cy_r, ow_s, ow_r, oy_s, oy_r, sum_s, sum_r, gr_s, gr_r, one_s, one_r,
):
    d = lax.axis_index("dp")
    s = lax.axis_index("space")
    c = lax.div(s, 2)
    k = lax.rem(s, 2)
    lin = d * 2 + k
    z = lax.div(c, 2)
    column_y = lax.rem(c, 2)
    across = lax.div(d, 4)
    along = lax.rem(d, 4)
    partner = {"space": c * 2 + 1 - k}

    def lanes(chip):
        return pl.ds(pl.multiple_of(chip * PAIR, PAIR), PAIR)

    def rows(index, size):
        return pl.ds(pl.multiple_of(index * size, size), size)

    def to(i):
        return lax.rem(s + i, SPACE)

    def frm(i):
        return lax.rem(s + SPACE - i, SPACE)

    def chip_to(i):
        return lax.rem(c + i, CHIPS)

    def chip_frm(i):
        return lax.rem(c + CHIPS - i, CHIPS)

    def each(count, body):
        def step(i, carry):
            body(i)
            return carry

        lax.fori_loop(1, count, step, 0)

    def take(ref, sem):
        pltpu.make_async_copy(ref, ref, sem).wait()

    def remote(src, dst, send, recv, where):
        return pltpu.make_async_remote_copy(
            src_ref=src, dst_ref=dst, send_sem=send, recv_sem=recv,
            device_id=where, device_id_type=MESH,
        )

    local = [
        pltpu.make_async_copy(w_ref, w, loc.at[0]),
        pltpu.make_async_copy(cot_ref.at[k], cext.at[pl.ds(pl.multiple_of(GRID + k * HERE, GRID), HERE)], loc.at[1]),
        pltpu.make_async_copy(cot_ref.at[k], cot_all.at[rows(k * SPACE + s, HERE)], loc.at[2]),
        pltpu.make_async_copy(q_ref.at[k, :, lanes(c)], qkv.at[0, rows(s, HERE)], loc.at[3]),
        pltpu.make_async_copy(k_ref.at[k, :, lanes(c)], qkv.at[1, rows(s, HERE)], loc.at[4]),
        pltpu.make_async_copy(v_ref.at[k, :, lanes(c)], qkv.at[2, rows(s, HERE)], loc.at[5]),
        pltpu.make_async_copy(table_ref, table, loc.at[6]),
        pltpu.make_async_copy(wc_ref, wc, loc.at[7]),
    ]
    for copy in local:
        copy.start()

    barrier = pltpu.get_barrier_semaphore()

    def greet(i):
        pl.semaphore_signal(barrier, inc=1, device_id={"space": to(i)}, device_id_type=MESH)
        other = lax.rem(lin + i, SPACE)
        pl.semaphore_signal(
            barrier, inc=1,
            device_id={"dp": lax.div(other, 2), "space": c * 2 + lax.rem(other, 2)},
            device_id_type=MESH,
        )

    each(SPACE, greet)
    pl.semaphore_wait(barrier, 2 * (SPACE - 1))

    halo = remote(
        cot_ref.at[1 - k], cext.at[pl.ds(pl.multiple_of(GRID + k * HERE, GRID), HERE)],
        halo_s.at[0], halo_r.at[0], partner,
    )
    halo.start()
    low_end = pl.ds(0, GRID)
    high_end = pl.ds(GRID + PAIR, GRID)

    def edge(core, begin, place, slot, chip):
        return remote(
            cot_ref.at[core, pl.ds(begin, GRID)], cext.at[place],
            halo_s.at[1 + core], halo_r.at[slot], {"space": chip * 2 + core},
        )

    @pl.when((k == 1) & (c < CHIPS - 1))
    def _():
        for core in range(2):
            edge(core, GRID, low_end, 1, c + 1).start()

    @pl.when((k == 0) & (c > 0))
    def _():
        for core in range(2):
            edge(core, 0, high_end, 2, c - 1).start()

    @pl.when(c == 0)
    def _():
        cext[low_end] = jnp.zeros((GRID, COUT), BF)

    @pl.when(c == CHIPS - 1)
    def _():
        cext[high_end] = jnp.zeros((GRID, COUT), BF)

    def send_qkv(i):
        peer = to(i)
        chip = lax.div(peer, 2)
        core = lax.rem(peer, 2)
        for j, ref in enumerate((q_ref, k_ref, v_ref)):
            remote(
                ref.at[core, :, lanes(chip)], qkv.at[j, rows(s, HERE)],
                qkv_s.at[i], qkv_r.at[i], {"space": peer},
            ).start()

    each(SPACE, send_qkv)

    def near(core, step):
        chip = z * 2 + lax.rem(column_y + step, 2)
        return remote(
            cot_ref.at[core], cot_all.at[rows(core * SPACE + s, HERE)],
            near_s.at[core, step], near_r.at[k, step], {"space": chip * 2 + core},
        )

    for core in range(2):
        near(core, 1).start()

        @pl.when(core != k)
        def _():
            near(core, 0).start()

    local[0].wait()
    local[6].wait()
    bias_here = table[pl.ds(step_ref[k], 1), :]
    high = bias_here.astype(BF)
    rest = bias_here - high.astype(F32)
    mid = rest.astype(BF)
    low = (rest - mid.astype(F32)).astype(BF)
    pieces = jnp.concatenate(
        [high.astype(F32), mid.astype(F32), low.astype(F32), jnp.zeros((13, CH), F32)], axis=0
    ).astype(BF)

    def permute(i, carry):
        n = lax.broadcasted_iota(jnp.int32, (BLOCK, CH), 0) + i * BLOCK
        e = lax.broadcasted_iota(jnp.int32, (BLOCK, CH), 1)
        n_chip = lax.shift_right_logical(n, 7)
        n_core = lax.shift_right_logical(n, 6) & 1
        n_dp = lax.shift_right_logical(n, 3) & 7
        target = n_dp * 128 + n_chip * 16 + n_core * 8 + (n & 7)
        pick = jnp.where(e == target, 1.0, 0.0).astype(BF)
        wperm[rows(i, BLOCK), :] = mm_nt(pick, w[...]).astype(BF)
        column = jnp.sum(mm_nt(pick, pieces), axis=1, keepdims=True)
        bias_col[rows(i, BLOCK), :] = jnp.broadcast_to(column, (BLOCK, PAIR))
        return carry

    lax.fori_loop(0, CH // BLOCK, permute, 0)

    local[1].wait()
    local[7].wait()
    halo.wait_send()
    take(cext.at[pl.ds(0, HERE)], halo_r.at[0])

    @pl.when(c > 0)
    def _():
        take(cext.at[low_end], halo_r.at[1])

    @pl.when(c < CHIPS - 1)
    def _():
        take(cext.at[high_end], halo_r.at[2])

    sums = []
    for col in range(3):
        total = None
        for row in range(3):
            start = 2 * GRID - GRID * row
            part = mm_nt(cext[start : start + PAIR, :], wc[3 * row + col])
            total = part if total is None else total + part
        sums.append(total)
    column = lax.broadcasted_iota(jnp.int32, (PAIR, CH), 0) & (GRID - 1)
    hidden_grad = (
        sums[1]
        + jnp.where(column < GRID - 1, pltpu.roll(sums[0], PAIR - 1, 0), 0.0)
        + jnp.where(column > 0, pltpu.roll(sums[2], 1, 0), 0.0)
    )
    hg_tok[...] = hidden_grad.astype(BF)
    ag_tok[...] = mm_nt(hg_tok[...], w[...]).astype(BF)

    def send_ag(i):
        chip = chip_to(i)
        remote(
            ag_tok.at[:, lanes(chip)], do.at[rows(c, PAIR)],
            ag_s.at[i], ag_r.at[i], {"space": chip * 2 + k},
        ).start()

    each(CHIPS, send_ag)
    do[rows(c, PAIR), :] = ag_tok[:, lanes(c)]

    for copy in local[3:6]:
        copy.wait()
    each(SPACE, lambda i: take(qkv.at[:, rows(frm(i), HERE), :], qkv_r.at[i]))

    def quarter(zz):
        return cot_all.at[pl.ds(pl.multiple_of(k * TOKENS + zz * 2 * PAIR, PAIR), 2 * PAIR)]

    def eighth(zz, part):
        begin = k * TOKENS + zz * 2 * PAIR + part * PAIR
        return cot_all.at[pl.ds(pl.multiple_of(begin, PAIR), PAIR)]

    z_up = lax.rem(z + 1, 4)
    z_down = lax.rem(z + 3, 4)
    up = {"space": (z_up * 2 + column_y) * 2 + k}
    down = {"space": (z_down * 2 + column_y) * 2 + k}
    small = cot_all.at[pl.ds(0, HERE)]
    local[2].wait()
    take(small, near_r.at[1 - k, 0])
    take(small, near_r.at[0, 1])
    take(small, near_r.at[1, 1])
    ring = [
        remote(quarter(z), quarter(z), cot_s.at[0], cot_r.at[0], up),
        remote(quarter(z), quarter(z), cot_s.at[1], cot_r.at[1], down),
        remote(eighth(z_down, 0), eighth(z_down, 0), cot_s.at[2], cot_r.at[2], up),
        remote(eighth(z_up, 1), eighth(z_up, 1), cot_s.at[3], cot_r.at[3], down),
    ]
    ring[0].start()
    ring[1].start()
    first = lax.broadcasted_iota(jnp.int32, (TOKENS, PAIR), 1) < HEAD_DIM
    key = qkv[1]
    km[0] = jnp.where(first, key, jnp.zeros_like(key))
    km[1] = jnp.where(first, jnp.zeros_like(key), key)
    kt[...] = key.astype(F32).T.astype(BF)
    vt[...] = qkv[2].astype(F32).T.astype(BF)

    def forward(i, carry):
        here = rows(i, BLOCK)
        query = qkv[0, here, :] * jnp.asarray(SCALE, BF)
        outs = []
        for h in range(2):
            scores = mm_nt(km[h], query)
            top = jnp.max(scores, axis=0, keepdims=True)
            shifted = jnp.exp(scores - top)
            total = jnp.sum(shifted, axis=0, keepdims=True)
            prob = shifted * (1.0 / total)
            probs[h, :, here] = prob
            outs.append(mm(vt[h * HEAD_DIM : (h + 1) * HEAD_DIM, :], prob.astype(BF)))
        out = jnp.concatenate(outs, axis=0)
        ot[:, here] = out.astype(BF)
        att[here, :] = out.T.astype(BF)
        for half in range(2):
            chip = 2 * i + half

            @pl.when(chip != c)
            def _():
                remote(
                    att.at[rows(chip, PAIR)], att_tok.at[:, lanes(c)],
                    att_s.at[chip], att_r.at[c], {"space": chip * 2 + k},
                ).start()

        return carry

    lax.fori_loop(0, TOKENS // BLOCK, forward, 0)
    att_tok[:, lanes(c)] = att[rows(c, PAIR), :]

    each(CHIPS, lambda i: take(do.at[rows(chip_frm(i), PAIR)], ag_r.at[i]))
    grad = do[...]
    dom[0] = jnp.where(first, grad, jnp.zeros_like(grad))
    dom[1] = jnp.where(first, jnp.zeros_like(grad), grad)
    dv_acc[...] = jnp.zeros_like(dv_acc)
    dk_acc[...] = jnp.zeros_like(dk_acc)

    def backward(i, carry):
        here = rows(i, BLOCK)
        query = qkv[0, here, :] * jnp.asarray(SCALE, BF)
        half = lax.broadcasted_iota(jnp.int32, (BLOCK, PAIR), 1) < HEAD_DIM
        product = ot[:, here].astype(F32) * do[here, :].astype(F32).T
        outs = []
        for h in range(2):
            prob = probs[h, :, here]
            grad_block = dom[h, here, :]
            dv_acc[...] += mm(prob.astype(BF), grad_block)
            prob_grad = mm_nt(qkv[2], grad_block)
            delta = jnp.sum(product[h * HEAD_DIM : (h + 1) * HEAD_DIM], axis=0, keepdims=True)
            score_grad = (prob * (prob_grad - delta)).astype(BF)
            zero = jnp.zeros_like(query)
            masked = jnp.where(half, query, zero) if h == 0 else jnp.where(half, zero, query)
            dk_acc[...] += mm(score_grad, masked)
            outs.append(mm(kt[h * HEAD_DIM : (h + 1) * HEAD_DIM, :], score_grad))
        gh[0, here, :] = (jnp.concatenate(outs, axis=0) * SCALE).T.astype(BF)
        return carry

    lax.fori_loop(0, SPLIT, backward, 0)

    take(quarter(z_down), cot_r.at[0])
    ring[2].start()
    take(quarter(z_up), cot_r.at[1])
    ring[3].start()

    each(CHIPS, lambda i: take(att_tok.at[:, lanes(chip_frm(i))], att_r.at[chip_frm(i)]))
    hsend[...] = (mm_nt(wperm[...], att_tok[...]) + bias_col[...]).astype(BF)

    def send_hidden(i):
        peer = to(i)
        remote(
            hsend.at[rows(peer, OWN)], hbuf.at[:, lanes(k * CHIPS + c)],
            hid_s.at[i], hid_r.at[i], {"space": peer},
        ).start()

    each(SPACE, send_hidden)
    hbuf[:, lanes(k * CHIPS + c)] = hsend[rows(s, OWN), :]

    flipped = att_tok[...].astype(F32).T.reshape(DP, CHIPS, 2, SLAB, PAIR)
    for core in range(2):
        for xx in range(4):
            for yy in range(2):
                at = (xx * 2 + yy) * HERE
                rows_of = flipped[yy * 4 + xx, :, core].reshape(HERE, PAIR)
                ow_lhs[core, at : at + HERE, :] = rows_of.astype(BF)

    def pass_on(i, carry):
        ow_pass[rows(i, PAIR), :] = mm(ow_lhs[1 - k, rows(i, PAIR), :], hg_tok[...]).astype(BF)
        return carry

    lax.fori_loop(0, 4, pass_on, 0)
    ow_copy = remote(ow_pass, ow_in, one_s.at[1], one_r.at[1], partner)
    ow_copy.start()

    lax.fori_loop(SPLIT, TOKENS // BLOCK, backward, 0)
    gh[1] = dk_acc[...].astype(BF)
    gh[2] = dv_acc[...].astype(BF)

    ow_copy.wait()

    def join(i, carry):
        both = mm(ow_lhs[k, rows(i, PAIR), :], hg_tok[...]) + ow_in[rows(i, PAIR), :].astype(F32)
        ow_send[rows(i, PAIR), :] = both.astype(BF)
        return carry

    lax.fori_loop(0, 4, join, 0)

    def send_ow(i):
        dest = lax.rem(along + i, 4)
        remote(
            ow_send.at[rows(dest, PAIR)], ow_recv.at[i], ow_s.at[i], ow_r.at[i],
            {"dp": across * 4 + dest},
        ).start()

    each(4, send_ow)

    z_far = lax.rem(z + 2, 4)
    take(eighth(z_far, 0), cot_r.at[2])
    take(eighth(z_far, 1), cot_r.at[3])
    mine = rows(k, TOKENS)
    cot_copy = remote(cot_all.at[mine], cot_all.at[mine], one_s.at[0], one_r.at[0], partner)
    cot_copy.start()

    def send_grads(i):
        peer = to(i)
        remote(
            gh.at[:, rows(peer, HERE), :], grads_ref.at[:, k, :, lanes(c)],
            gr_s.at[i], gr_r.at[i], {"space": peer},
        ).start()

    each(SPACE, send_grads)
    own_grads = pltpu.make_async_copy(
        gh.at[:, rows(s, HERE), :], grads_ref.at[:, k, :, lanes(c)], loc.at[0]
    )
    own_grads.start()

    def take_hidden(i):
        peer = frm(i)
        take(hbuf.at[:, lanes(lax.rem(peer, 2) * CHIPS + lax.div(peer, 2))], hid_r.at[i])

    each(SPACE, take_hidden)

    spot = lax.broadcasted_iota(jnp.int32, (OWN, TOKENS), 1)
    y = lax.shift_right_logical(spot, 5)
    x = spot & (GRID - 1)
    for sample in range(2):
        hidden = hbuf[:, sample * TOKENS : (sample + 1) * TOKENS].astype(F32)
        for row in range(3):
            for col in range(3):
                offset = (row - 1) * GRID + col - 1
                moved = pltpu.roll(hidden, (-offset) % TOKENS, 1) if offset else hidden
                good = None
                for ok in (
                    [y > 0] * (row == 0) + [y < GRID - 1] * (row == 2)
                    + [x > 0] * (col == 0) + [x < GRID - 1] * (col == 2)
                ):
                    good = ok if good is None else good & ok
                if good is not None:
                    moved = jnp.where(good, moved, 0.0)
                tap = 3 * row + col
                lhs[sample, tap * OWN : (tap + 1) * OWN, :] = moved.astype(BF)
        lhs[sample, TAPS * OWN :, :] = jnp.zeros((OWN, TOKENS), BF)
    tiles = [(at, min(at + BLOCK, COUT)) for at in range(0, COUT, BLOCK)]
    for at, end in tiles:
        conv_acc[:, at:end] = mm(lhs[k], cot_all[mine, at:end])
    cot_copy.wait_send()
    other = rows(1 - k, TOKENS)
    take(cot_all.at[other], one_r.at[0])
    for tile, (at, end) in enumerate(tiles):
        part = conv_acc[:, at:end] + mm(lhs[1 - k], cot_all[other, at:end])
        for dest in range(DP):
            for pair in range(5):
                top = pair * 2 * OWN + dest * SLAB
                both = jnp.concatenate(
                    [part[top : top + SLAB], part[top + OWN : top + OWN + SLAB]], axis=0
                )
                conv_send[dest % 4, dest // 4, pair * 16 : pair * 16 + 16, at:end] = both.astype(BF)

        def send_conv(i):
            dest = lax.rem(along + i, 4)
            remote(
                conv_send.at[dest, :, :, at:end], conv_recv.at[i, :, :, at:end],
                conv_s.at[tile, i], conv_r.at[tile, i], {"dp": across * 4 + dest},
            ).start()

        each(4, send_conv)

    opposite = {"dp": lax.rem(d + 4, DP)}
    each(4, lambda i: take(ow_recv.at[i], ow_r.at[i]))
    total = ow_send[rows(along, PAIR), :].astype(F32)
    for i in range(1, 4):
        total = total + ow_recv[i].astype(F32)
    ow_keep[...] = total
    ow_out[...] = ow_keep[rows(1 - across, HERE), :].astype(BF)
    ow_turn = remote(ow_out, ow_back, oy_s.at[0], oy_r.at[0], opposite)
    ow_turn.start()

    turns = []
    for tile, (at, end) in enumerate(tiles):
        each(4, lambda i: take(conv_recv.at[i, :, :, at:end], conv_r.at[tile, i]))
        for half in range(2):
            total = conv_send[along, half, :, at:end].astype(F32)
            for i in range(1, 4):
                total = total + conv_recv[i, half, :, at:end].astype(F32)
            conv_keep[half, :, at:end] = total
        conv_out[:, at:end] = conv_keep[1 - across, :, at:end].astype(BF)
        turn = remote(
            conv_out.at[:, at:end], conv_in.at[:, at:end], cy_s.at[tile], cy_r.at[tile], opposite
        )
        turn.start()
        turns.append(turn)

    ow_turn.wait()
    ow_sum[...] = ow_keep[rows(across, HERE), :] + ow_back[...].astype(F32)

    def send_sum(i):
        chip = chip_to(i)
        remote(
            ow_sum.at[rows(chip, SLAB)], ow_parts.at[i],
            sum_s.at[i], sum_r.at[i], {"space": chip * 2 + k},
        ).start()

    each(CHIPS, send_sum)

    for tile, (at, end) in enumerate(tiles):
        turns[tile].wait()
        total = conv_keep[across, :, at:end] + conv_in[:, at:end].astype(F32)
        for tap in range(TAPS):
            gc_ref[tap, :, at:end] = total[tap * SLAB : (tap + 1) * SLAB]

    each(CHIPS, lambda i: take(ow_parts.at[i], sum_r.at[i]))
    total = ow_sum[rows(c, SLAB), :]
    for i in range(1, CHIPS):
        total = total + ow_parts[i]
    gw_ref[...] = total

    own_grads.wait()

    def take_grads(i):
        peer = frm(i)
        take(grads_ref.at[:, lax.rem(peer, 2), :, lanes(lax.div(peer, 2))], gr_r.at[i])

    each(SPACE, take_grads)

    def sent(i):
        take(qkv.at[:, rows(0, HERE), :], qkv_s.at[i])
        take(hsend.at[rows(0, OWN)], hid_s.at[i])
        take(gh.at[:, rows(0, HERE), :], gr_s.at[i])

    each(SPACE, sent)

    def sent_chips(i):
        take(att.at[rows(0, PAIR)], att_s.at[chip_to(i)])
        take(ag_tok.at[:, lanes(0)], ag_s.at[i])
        take(ow_sum.at[rows(0, SLAB)], sum_s.at[i])

    each(CHIPS, sent_chips)

    def sent_along(i):
        take(ow_send.at[rows(0, PAIR)], ow_s.at[i])
        for tile, (at, end) in enumerate(tiles):
            take(conv_send.at[0, :, :, at:end], conv_s.at[tile, i])

    each(4, sent_along)
    for copy in ring:
        copy.wait_send()
    for core in range(2):
        take(small, near_s.at[core, 1])
    take(small, near_s.at[1 - k, 0])

    @pl.when(((k == 1) & (c < CHIPS - 1)) | ((k == 0) & (c > 0)))
    def _():
        for core in range(2):
            take(cext.at[low_end], halo_s.at[1 + core])


def hand_over(*refs):
    sources, outs, held, sems = refs[:3], refs[3:8], refs[8:13], refs[13]
    grads_ref, gw_ref, gc_ref = sources
    ins = [grads_ref.at[0], grads_ref.at[1], grads_ref.at[2], gw_ref, gc_ref]
    arrive = [pltpu.make_async_copy(a, b, sems.at[0, j]) for j, (a, b) in enumerate(zip(ins, held))]
    leave = [pltpu.make_async_copy(a, b, sems.at[1, j]) for j, (a, b) in enumerate(zip(held, outs))]
    for copy in arrive:
        copy.start()
    for first, second in zip(arrive, leave):
        first.wait()
        second.start()
    for copy in leave:
        copy.wait()


def on_device(queries, keys, values, cotangent, timesteps, time_table, out_weight, conv_weight):
    anywhere = pl.BlockSpec(memory_space=pl.ANY)
    vmem = pl.BlockSpec(memory_space=pltpu.VMEM)
    sems = pltpu.SemaphoreType.DMA
    wide = jax.ShapeDtypeStruct((2, HERE, CH), BF)
    gw_shape = jax.ShapeDtypeStruct((SLAB, CH), F32)
    gc_shape = jax.ShapeDtypeStruct((TAPS, SLAB, COUT), F32)
    parts = pl.pallas_call(
        kernel,
        out_shape=(jax.ShapeDtypeStruct((3, 2, HERE, CH), BF), gw_shape, gc_shape),
        in_specs=[anywhere] * 7 + [pl.BlockSpec(memory_space=pltpu.SMEM)],
        out_specs=(anywhere, vmem, vmem),
        scratch_shapes=[
            pltpu.VMEM((3, TOKENS, PAIR), BF),
            pltpu.VMEM((2 * TOKENS, COUT), BF),
            pltpu.VMEM((PAIR + 2 * GRID, COUT), BF),
            pltpu.VMEM((CH, CH), BF),
            pltpu.VMEM((TAPS, CH, COUT), BF),
            pltpu.VMEM((STEPS, CH), F32),
            pltpu.VMEM((CH, CH), BF),
            pltpu.VMEM((CH, PAIR), F32),
            pltpu.VMEM((2, TOKENS, PAIR), BF),
            pltpu.VMEM((2, TOKENS, PAIR), BF),
            pltpu.VMEM((PAIR, TOKENS), BF),
            pltpu.VMEM((PAIR, TOKENS), BF),
            pltpu.VMEM((2, TOKENS, TOKENS), F32),
            pltpu.VMEM((PAIR, TOKENS), BF),
            pltpu.VMEM((TOKENS, PAIR), BF),
            pltpu.VMEM((PAIR, CH), BF),
            pltpu.VMEM((PAIR, CH), BF),
            pltpu.VMEM((PAIR, CH), BF),
            pltpu.VMEM((CH, PAIR), BF),
            pltpu.VMEM((OWN, 2 * TOKENS), BF),
            pltpu.VMEM((2, 10 * OWN, TOKENS), BF),
            pltpu.VMEM((10 * OWN, COUT), F32),
            pltpu.VMEM((4, 2, ROWS, COUT), BF),
            pltpu.VMEM((4, 2, ROWS, COUT), BF),
            pltpu.VMEM((2, ROWS, COUT), F32),
            pltpu.VMEM((ROWS, COUT), BF),
            pltpu.VMEM((ROWS, COUT), BF),
            pltpu.VMEM((TOKENS, PAIR), BF),
            pltpu.VMEM((TOKENS, PAIR), F32),
            pltpu.VMEM((TOKENS, PAIR), F32),
            pltpu.VMEM((3, TOKENS, PAIR), BF),
            pltpu.VMEM((2, CH // 2, PAIR), BF),
            pltpu.VMEM((CH // 2, CH), BF),
            pltpu.VMEM((CH // 2, CH), BF),
            pltpu.VMEM((CH // 2, CH), BF),
            pltpu.VMEM((4, PAIR, CH), BF),
            pltpu.VMEM((PAIR, CH), F32),
            pltpu.VMEM((HERE, CH), BF),
            pltpu.VMEM((HERE, CH), BF),
            pltpu.VMEM((HERE, CH), F32),
            pltpu.VMEM((CHIPS, SLAB, CH), F32),
            sems((8,)),
            sems((3,)), sems((3,)),
            sems((SPACE,)), sems((SPACE,)),
            sems((2, 2)), sems((2, 2)),
            sems((4,)), sems((4,)),
            sems((CHIPS,)), sems((CHIPS,)),
            sems((CHIPS,)), sems((CHIPS,)),
            sems((SPACE,)), sems((SPACE,)),
            sems((3, 4)), sems((3, 4)),
            sems((3,)), sems((3,)),
            sems((4,)), sems((4,)),
            sems((1,)), sems((1,)),
            sems((CHIPS,)), sems((CHIPS,)),
            sems((SPACE,)), sems((SPACE,)),
            sems((2,)), sems((2,)),
        ],
        compiler_params=pltpu.CompilerParams(
            collective_id=0, has_side_effects=True, vmem_limit_bytes=60 * 1024 * 1024
        ),
        cost_estimate=pl.CostEstimate(
            flops=8_000_000_000, bytes_accessed=20_000_000, transcendentals=2_000_000
        ),
    )(
        queries, keys, values, cotangent, out_weight, jnp.transpose(conv_weight, (1, 0, 2)),
        time_table, timesteps,
    )
    gq, gk, gv, gw, gc = pl.pallas_call(
        hand_over,
        out_shape=(wide, wide, wide, gw_shape, gc_shape),
        in_specs=[anywhere] * 3,
        out_specs=(anywhere,) * 5,
        scratch_shapes=[pltpu.VMEM((2, HERE, CH), BF)] * 3
        + [pltpu.VMEM((SLAB, CH), F32), pltpu.VMEM((TAPS, SLAB, COUT), F32), sems((2, 5))],
    )(*parts)
    return gq, gk, gv, gw, jnp.transpose(gc, (1, 0, 2))


def solution(mesh):
    return jax.shard_map(
        on_device,
        mesh=mesh,
        in_specs=(
            P("dp", "space", None),
            P("dp", "space", None),
            P("dp", "space", None),
            P("dp", "space", None),
            P("dp"),
            P(),
            P(),
            P(),
        ),
        out_specs=(
            P("dp", "space", None),
            P("dp", "space", None),
            P("dp", "space", None),
            P(("dp", "space"), None),
            P(("dp", "space"), None, None),
        ),
        check_vma=False,
    )
```

time: 114 us -> 76.9 us (0.67)
  the two profiles are of different devices: /device:TPU:40 before, /device:TPU:0 now
where the time goes in v2:
time: 76.9 us; the launch traced here: 76.8 us
  Pallas kernels  76.1 us (99%)
    pallas_call x1, Pallas kernels, on_device(): pl.pallas_call(kernel, out_shape=(jax.ShapeDtypeStruct((3, 2, HERE, CH),...  74.2 us
    pallas_call x1, Pallas kernels, on_device(): pl.pallas_call(hand_over, out_shape=(wide, wide, wide, gw_shape, gc_shape...  1.98 us

profile of v2, /device:TPU:0, one launch (start us, length us, event | category | flops | bytes accessed | tf_op | source)
XLA Modules:
  0.0 76.8 jit_solution(7489357013844027916)
XLA Ops:
  0.6 74.2 %shard_map.119 = (bf16[3,2,64,1024]{3,2,1,0:T(8,128)(2,1)}, f32[8,1024]{1,0:T(8,128)}, f32[9,8,640]{2,1,0:T(8,128)}) custom-call(bf16[2,64,1024]{2,1,0:T(8,128)(2,1)} %q_ref.1, bf16[2,64,1024]{2,1,0:T(8,128)(2,1)} %k_ref.1, bf16[2,64,1024]{2,1,0:T(8,128)(2,1)} %v_ref.1, bf16[2,64,640]{2,1,0:T(8,128)(2,1)} %cot_ref.1, bf16[1024,1024]{1,0:T(8,128)(2,1)} %w_ref.1, ...), custom_call_target="tpu_custom_call" | custom-call | flops 8000000000 | bytes 20000000 | tf_op jit(solution)/shard_map/pallas_call | solution.py:577
  74.8 2.0 %shard_map.120 = (bf16[2,64,1024]{2,1,0:T(8,128)(2,1)}, bf16[2,64,1024]{2,1,0:T(8,128)(2,1)}, bf16[2,64,1024]{2,1,0:T(8,128)(2,1)}, f32[8,1024]{1,0:T(8,128)}, f32[9,8,640]{2,1,0:T(8,128)}) custom-call(bf16[3,2,64,1024]{3,2,1,0:T(8,128)(2,1)} %get-tuple-element.13.refs_0_, f32[8,1024]{1,0:T(8,128)} %get-tuple-element.14.refs_1_, ...), custom_call_target="tpu_custom_call" | custom-call | tf_op jit(solution)/shard_map/pallas_call | solution.py:650

commit v3 on v2

--- a/solution.py
+++ b/solution.py
@@ -20,8 +20,8 @@
 OWN = DP * SLAB
 ROWS = 80
 BLOCK = 256
-SPLIT = 2
 STEPS = 1000
+HALF = CH // 2
 SCALE = HEAD_DIM ** (-0.5)
 MESH = pl.DeviceIdType.MESH
 NT = (((1,), (1,)), ((), ()))
@@ -40,11 +40,11 @@
 def kernel(
     q_ref, k_ref, v_ref, cot_ref, w_ref, wc_ref, table_ref, step_ref,
     grads_ref, gw_ref, gc_ref,
-    qkv, cot_all, cext, w, wc, table, wperm, bias_col, km, dom, vt, kt, probs, ot, att, att_tok,
-    hg_tok, ag_tok, hsend, hbuf, lhs, conv_acc, conv_send, conv_recv, conv_keep, conv_out, conv_in, do, dv_acc, dk_acc, gh,
-    ow_lhs, ow_pass, ow_in, ow_send, ow_recv, ow_keep, ow_out, ow_back, ow_sum, ow_parts,
-    loc, halo_s, halo_r, qkv_s, qkv_r, near_s, near_r, cot_s, cot_r, ag_s, ag_r, att_s, att_r, hid_s, hid_r,
-    conv_s, conv_r, cy_s, cy_r, ow_s, ow_r, oy_s, oy_r, sum_s, sum_r, gr_s, gr_r, one_s, one_r,
+    qkv, cot_all, cext, w, wc, table, wperm, bias_col, qm, dom, vt, kt, probs, ot, att, att_tok,
+    hg_tok, ag_tok, hsend, hbuf, lhs, conv_acc, conv_send, conv_recv, conv_keep, conv_out, conv_in, do, delta, dq_acc, gh,
+    ow_lhs, ow_pass, ow_in, ow_send, ow_recv, ow_keep, ow_x, ow_xr, ow_y, ow_parts,
+    loc, halo_s, halo_r, qkv_s, qkv_r, near_s, near_r, cot_s, cot_r, hop_s, hop_r, share_s, share_r, ag_s, ag_r, att_s, att_r, hid_s, hid_r,
+    conv_s, conv_r, cy_s, cy_r, ow_s, ow_r, ox_s, ox_r, oy_s, oy_r, gr_s, gr_r, gq_s, gq_r, one_s, one_r,
 ):
     d = lax.axis_index("dp")
     s = lax.axis_index("space")
@@ -116,7 +116,9 @@
         )
 
     each(SPACE, greet)
-    pl.semaphore_wait(barrier, 2 * (SPACE - 1))
+    diagonal = {"dp": lax.rem(d + 4, DP), "space": (z * 2 + 1 - column_y) * 2 + k}
+    pl.semaphore_signal(barrier, inc=1, device_id=diagonal, device_id_type=MESH)
+    pl.semaphore_wait(barrier, 2 * (SPACE - 1) + 1)
 
     halo = remote(
         cot_ref.at[1 - k], cext.at[pl.ds(pl.multiple_of(GRID + k * HERE, GRID), HERE)],
@@ -150,17 +152,18 @@
     def _():
         cext[high_end] = jnp.zeros((GRID, COUT), BF)
 
-    def send_qkv(i):
+    def send_heads(i, arrays, sem):
         peer = to(i)
         chip = lax.div(peer, 2)
         core = lax.rem(peer, 2)
-        for j, ref in enumerate((q_ref, k_ref, v_ref)):
+        for j, ref in arrays:
             remote(
                 ref.at[core, :, lanes(chip)], qkv.at[j, rows(s, HERE)],
-                qkv_s.at[i], qkv_r.at[i], {"space": peer},
+                qkv_s.at[sem], qkv_r.at[sem], {"space": peer},
             ).start()
 
-    each(SPACE, send_qkv)
+    each(SPACE, lambda i: send_heads(i, ((0, q_ref), (1, k_ref)), 0))
+    each(SPACE, lambda i: send_heads(i, ((2, v_ref),), 1))
 
     def near(core, step):
         chip = z * 2 + lax.rem(column_y + step, 2)
@@ -175,6 +178,14 @@
         @pl.when(core != k)
         def _():
             near(core, 0).start()
+
+    for i, (shift_z, shift_y) in enumerate(((1, 0), (3, 0), (2, 0), (2, 1)), 1):
+        chip = lax.rem(z + shift_z, 4) * 2 + lax.rem(column_y + shift_y, 2)
+        for core in range(2):
+            remote(
+                cot_ref.at[core], cot_all.at[rows(core * SPACE + s, HERE)],
+                cot_s.at[i, core], cot_r.at[i, k], {"space": chip * 2 + core},
+            ).start()
 
     local[0].wait()
     local[6].wait()
@@ -236,59 +247,73 @@
         chip = chip_to(i)
         remote(
             ag_tok.at[:, lanes(chip)], do.at[rows(c, PAIR)],
-            ag_s.at[i], ag_r.at[i], {"space": chip * 2 + k},
+            ag_s.at[0], ag_r.at[0], {"space": chip * 2 + k},
         ).start()
 
-    each(CHIPS, send_ag)
-    do[rows(c, PAIR), :] = ag_tok[:, lanes(c)]
-
+
+    most = pl.ds(0, TOKENS - HERE)
+    chips = pl.ds(0, TOKENS - PAIR)
     for copy in local[3:6]:
         copy.wait()
-    each(SPACE, lambda i: take(qkv.at[:, rows(frm(i), HERE), :], qkv_r.at[i]))
-
-    def quarter(zz):
-        return cot_all.at[pl.ds(pl.multiple_of(k * TOKENS + zz * 2 * PAIR, PAIR), 2 * PAIR)]
-
-    def eighth(zz, part):
-        begin = k * TOKENS + zz * 2 * PAIR + part * PAIR
-        return cot_all.at[pl.ds(pl.multiple_of(begin, PAIR), PAIR)]
+    take(qkv.at[pl.ds(0, 2), most], qkv_r.at[0])
+
+    def block(zz, yy):
+        return cot_all.at[pl.ds(pl.multiple_of(k * TOKENS + (zz * 2 + yy) * PAIR, PAIR), PAIR)]
 
     z_up = lax.rem(z + 1, 4)
     z_down = lax.rem(z + 3, 4)
-    up = {"space": (z_up * 2 + column_y) * 2 + k}
-    down = {"space": (z_down * 2 + column_y) * 2 + k}
+    z_far = lax.rem(z + 2, 4)
+    other_y = 1 - column_y
     small = cot_all.at[pl.ds(0, HERE)]
+    ring = []
+    for j, (zz, yy, chip) in enumerate((
+        (z, other_y, z_up * 2 + column_y),
+        (z, other_y, z_down * 2 + column_y),
+    )):
+        ring.append(
+            remote(
+                block(zz, yy), block(zz, yy), hop_s.at[j], hop_r.at[j], {"space": chip * 2 + k}
+            )
+        )
+    own_blocks = ((z, 0), (z, 1), (z_up, column_y), (z_down, column_y), (z_far, 0), (z_far, 1))
+    hop_blocks = ((z_down, other_y), (z_up, other_y))
+
+    def share(blocks, slot):
+        for zz, yy in blocks:
+            remote(
+                block(zz, yy), block(zz, yy), share_s.at[slot], share_r.at[slot], partner
+            ).start()
+
+    first = lax.broadcasted_iota(jnp.int32, (TOKENS, PAIR), 1) < HEAD_DIM
+    query = qkv[0] * jnp.asarray(SCALE, BF)
+    qm[0] = jnp.where(first, query, jnp.zeros_like(query))
+    qm[1] = jnp.where(first, jnp.zeros_like(query), query)
+
+    def weigh(i, carry):
+        here = rows(i, BLOCK)
+        for h in range(2):
+            scores = mm_nt(qkv[1], qm[h, here, :])
+            top = jnp.max(scores, axis=0, keepdims=True)
+            shifted = jnp.exp(scores - top)
+            total = jnp.sum(shifted, axis=0, keepdims=True)
+            probs[h, :, here] = (shifted * (1.0 / total)).astype(BF)
+        return carry
+
+    lax.fori_loop(0, TOKENS // BLOCK, weigh, 0)
     local[2].wait()
     take(small, near_r.at[1 - k, 0])
     take(small, near_r.at[0, 1])
     take(small, near_r.at[1, 1])
-    ring = [
-        remote(quarter(z), quarter(z), cot_s.at[0], cot_r.at[0], up),
-        remote(quarter(z), quarter(z), cot_s.at[1], cot_r.at[1], down),
-        remote(eighth(z_down, 0), eighth(z_down, 0), cot_s.at[2], cot_r.at[2], up),
-        remote(eighth(z_up, 1), eighth(z_up, 1), cot_s.at[3], cot_r.at[3], down),
-    ]
     ring[0].start()
     ring[1].start()
-    first = lax.broadcasted_iota(jnp.int32, (TOKENS, PAIR), 1) < HEAD_DIM
-    key = qkv[1]
-    km[0] = jnp.where(first, key, jnp.zeros_like(key))
-    km[1] = jnp.where(first, jnp.zeros_like(key), key)
-    kt[...] = key.astype(F32).T.astype(BF)
+    take(qkv.at[2, most], qkv_r.at[1])
     vt[...] = qkv[2].astype(F32).T.astype(BF)
 
     def forward(i, carry):
         here = rows(i, BLOCK)
-        query = qkv[0, here, :] * jnp.asarray(SCALE, BF)
-        outs = []
-        for h in range(2):
-            scores = mm_nt(km[h], query)
-            top = jnp.max(scores, axis=0, keepdims=True)
-            shifted = jnp.exp(scores - top)
-            total = jnp.sum(shifted, axis=0, keepdims=True)
-            prob = shifted * (1.0 / total)
-            probs[h, :, here] = prob
-            outs.append(mm(vt[h * HEAD_DIM : (h + 1) * HEAD_DIM, :], prob.astype(BF)))
+        outs = [
+            mm(vt[h * HEAD_DIM : (h + 1) * HEAD_DIM, :], probs[h, :, here]) for h in range(2)
+        ]
         out = jnp.concatenate(outs, axis=0)
         ot[:, here] = out.astype(BF)
         att[here, :] = out.T.astype(BF)
@@ -299,7 +324,7 @@
             def _():
                 remote(
                     att.at[rows(chip, PAIR)], att_tok.at[:, lanes(c)],
-                    att_s.at[chip], att_r.at[c], {"space": chip * 2 + k},
+                    att_s.at[0], att_r.at[0], {"space": chip * 2 + k},
                 ).start()
 
         return carry
@@ -307,116 +332,104 @@
     lax.fori_loop(0, TOKENS // BLOCK, forward, 0)
     att_tok[:, lanes(c)] = att[rows(c, PAIR), :]
 
-    each(CHIPS, lambda i: take(do.at[rows(chip_frm(i), PAIR)], ag_r.at[i]))
-    grad = do[...]
-    dom[0] = jnp.where(first, grad, jnp.zeros_like(grad))
-    dom[1] = jnp.where(first, jnp.zeros_like(grad), grad)
-    dv_acc[...] = jnp.zeros_like(dv_acc)
-    dk_acc[...] = jnp.zeros_like(dk_acc)
-
-    def backward(i, carry):
-        here = rows(i, BLOCK)
-        query = qkv[0, here, :] * jnp.asarray(SCALE, BF)
-        half = lax.broadcasted_iota(jnp.int32, (BLOCK, PAIR), 1) < HEAD_DIM
-        product = ot[:, here].astype(F32) * do[here, :].astype(F32).T
-        outs = []
-        for h in range(2):
-            prob = probs[h, :, here]
-            grad_block = dom[h, here, :]
-            dv_acc[...] += mm(prob.astype(BF), grad_block)
-            prob_grad = mm_nt(qkv[2], grad_block)
-            delta = jnp.sum(product[h * HEAD_DIM : (h + 1) * HEAD_DIM], axis=0, keepdims=True)
-            score_grad = (prob * (prob_grad - delta)).astype(BF)
-            zero = jnp.zeros_like(query)
-            masked = jnp.where(half, query, zero) if h == 0 else jnp.where(half, zero, query)
-            dk_acc[...] += mm(score_grad, masked)
-            outs.append(mm(kt[h * HEAD_DIM : (h + 1) * HEAD_DIM, :], score_grad))
-        gh[0, here, :] = (jnp.concatenate(outs, axis=0) * SCALE).T.astype(BF)
-        return carry
-
-    lax.fori_loop(0, SPLIT, backward, 0)
-
-    take(quarter(z_down), cot_r.at[0])
-    ring[2].start()
-    take(quarter(z_up), cot_r.at[1])
-    ring[3].start()
-
-    each(CHIPS, lambda i: take(att_tok.at[:, lanes(chip_frm(i))], att_r.at[chip_frm(i)]))
+    take(att.at[chips], att_r.at[0])
     hsend[...] = (mm_nt(wperm[...], att_tok[...]) + bias_col[...]).astype(BF)
 
     def send_hidden(i):
         peer = to(i)
         remote(
             hsend.at[rows(peer, OWN)], hbuf.at[:, lanes(k * CHIPS + c)],
-            hid_s.at[i], hid_r.at[i], {"space": peer},
+            hid_s.at[0], hid_r.at[0], {"space": peer},
         ).start()
 
     each(SPACE, send_hidden)
+    each(CHIPS, send_ag)
+    do[rows(c, PAIR), :] = ag_tok[:, lanes(c)]
     hbuf[:, lanes(k * CHIPS + c)] = hsend[rows(s, OWN), :]
 
     flipped = att_tok[...].astype(F32).T.reshape(DP, CHIPS, 2, SLAB, PAIR)
     for core in range(2):
-        for xx in range(4):
-            for yy in range(2):
-                at = (xx * 2 + yy) * HERE
-                rows_of = flipped[yy * 4 + xx, :, core].reshape(HERE, PAIR)
-                ow_lhs[core, at : at + HERE, :] = rows_of.astype(BF)
+        for zz in range(4):
+            for xx in range(4):
+                for yy in range(2):
+                    rows_of = flipped[yy * 4 + xx, 2 * zz : 2 * zz + 2, core].reshape(16, PAIR)
+                    rows_of = rows_of.astype(BF)
+                    for path, first_of in enumerate((xx * 4 + zz, zz * 4 + xx)):
+                        at = (first_of * 2 + yy) * 16
+                        ow_lhs[path, core, at : at + 16, :] = rows_of
 
     def pass_on(i, carry):
-        ow_pass[rows(i, PAIR), :] = mm(ow_lhs[1 - k, rows(i, PAIR), :], hg_tok[...]).astype(BF)
+        for path in range(2):
+            part = mm(ow_lhs[path, 1 - k, rows(i, PAIR), :], hg_tok[:, path * HALF : path * HALF + HALF])
+            ow_pass[path, rows(i, PAIR), :] = part.astype(BF)
         return carry
 
     lax.fori_loop(0, 4, pass_on, 0)
-    ow_copy = remote(ow_pass, ow_in, one_s.at[1], one_r.at[1], partner)
+    ow_copy = remote(ow_pass, ow_in, one_s.at[0], one_r.at[0], partner)
     ow_copy.start()
-
-    lax.fori_loop(SPLIT, TOKENS // BLOCK, backward, 0)
-    gh[1] = dk_acc[...].astype(BF)
-    gh[2] = dv_acc[...].astype(BF)
+    def by_x(i):
+        dest = lax.rem(along + i, 4)
+        return dest, {"dp": across * 4 + dest}
+
+    def by_z(i):
+        dest = lax.rem(z + i, 4)
+        return dest, {"space": (dest * 2 + column_y) * 2 + k}
+
+    def send_ow(path, way):
+        def one(i):
+            dest, where = way(i)
+            remote(
+                ow_send.at[path, rows(dest, PAIR)], ow_recv.at[path, i],
+                ow_s.at[path], ow_r.at[path], where,
+            ).start()
+
+        each(4, one)
+
+    def sum_ow(path, index):
+        take(ow_recv.at[path, pl.ds(1, 3)], ow_r.at[path])
+        total = ow_send[path, rows(index, PAIR), :].astype(F32)
+        for i in range(1, 4):
+            total = total + ow_recv[path, i].astype(F32)
+        ow_keep[path] = total
+        ow_x[path] = total.astype(BF)
+
+    def send_ow_on(path, way):
+        def one(i):
+            dest, where = way(i)
+            remote(
+                ow_x.at[path, rows(dest, GRID)], ow_xr.at[path, i],
+                ox_s.at[path], ox_r.at[path], where,
+            ).start()
+
+        each(4, one)
+
+    def sum_ow_on(path, index):
+        take(ow_xr.at[path, pl.ds(1, 3)], ox_r.at[path])
+        total = ow_keep[path, rows(index, GRID), :]
+        for i in range(1, 4):
+            total = total + ow_xr[path, i].astype(F32)
+        ow_y[:, path * HALF : path * HALF + HALF] = total
+
+    for i in range(1, 5):
+        for core in range(2):
+            take(small, cot_r.at[i, core])
+    share(own_blocks, 0)
 
     ow_copy.wait()
 
     def join(i, carry):
-        both = mm(ow_lhs[k, rows(i, PAIR), :], hg_tok[...]) + ow_in[rows(i, PAIR), :].astype(F32)
-        ow_send[rows(i, PAIR), :] = both.astype(BF)
+        for path in range(2):
+            part = mm(ow_lhs[path, k, rows(i, PAIR), :], hg_tok[:, path * HALF : path * HALF + HALF])
+            both = part + ow_in[path, rows(i, PAIR), :].astype(F32)
+            ow_send[path, rows(i, PAIR), :] = both.astype(BF)
         return carry
 
     lax.fori_loop(0, 4, join, 0)
 
-    def send_ow(i):
-        dest = lax.rem(along + i, 4)
-        remote(
-            ow_send.at[rows(dest, PAIR)], ow_recv.at[i], ow_s.at[i], ow_r.at[i],
-            {"dp": across * 4 + dest},
-        ).start()
-
-    each(4, send_ow)
-
-    z_far = lax.rem(z + 2, 4)
-    take(eighth(z_far, 0), cot_r.at[2])
-    take(eighth(z_far, 1), cot_r.at[3])
-    mine = rows(k, TOKENS)
-    cot_copy = remote(cot_all.at[mine], cot_all.at[mine], one_s.at[0], one_r.at[0], partner)
-    cot_copy.start()
-
-    def send_grads(i):
-        peer = to(i)
-        remote(
-            gh.at[:, rows(peer, HERE), :], grads_ref.at[:, k, :, lanes(c)],
-            gr_s.at[i], gr_r.at[i], {"space": peer},
-        ).start()
-
-    each(SPACE, send_grads)
-    own_grads = pltpu.make_async_copy(
-        gh.at[:, rows(s, HERE), :], grads_ref.at[:, k, :, lanes(c)], loc.at[0]
-    )
-    own_grads.start()
-
-    def take_hidden(i):
-        peer = frm(i)
-        take(hbuf.at[:, lanes(lax.rem(peer, 2) * CHIPS + lax.div(peer, 2))], hid_r.at[i])
-
-    each(SPACE, take_hidden)
+    send_ow(0, by_x)
+    send_ow(1, by_z)
+
+    take(hsend.at[most], hid_r.at[0])
 
     spot = lax.broadcasted_iota(jnp.int32, (OWN, TOKENS), 1)
     y = lax.shift_right_logical(spot, 5)
@@ -438,12 +451,19 @@
                 tap = 3 * row + col
                 lhs[sample, tap * OWN : (tap + 1) * OWN, :] = moved.astype(BF)
         lhs[sample, TAPS * OWN :, :] = jnp.zeros((OWN, TOKENS), BF)
+    for j in range(2):
+        take(block(0, 0), hop_r.at[j])
+    share(hop_blocks, 1)
+    mine = rows(k, TOKENS)
+
     tiles = [(at, min(at + BLOCK, COUT)) for at in range(0, COUT, BLOCK)]
     for at, end in tiles:
         conv_acc[:, at:end] = mm(lhs[k], cot_all[mine, at:end])
-    cot_copy.wait_send()
     other = rows(1 - k, TOKENS)
-    take(cot_all.at[other], one_r.at[0])
+    six = cot_all.at[pl.ds(0, 6 * PAIR)]
+    two = cot_all.at[pl.ds(0, 2 * PAIR)]
+    take(six, share_r.at[0])
+    take(two, share_r.at[1])
     for tile, (at, end) in enumerate(tiles):
         part = conv_acc[:, at:end] + mm(lhs[1 - k], cot_all[other, at:end])
         for dest in range(DP):
@@ -458,24 +478,75 @@
             dest = lax.rem(along + i, 4)
             remote(
                 conv_send.at[dest, :, :, at:end], conv_recv.at[i, :, :, at:end],
-                conv_s.at[tile, i], conv_r.at[tile, i], {"dp": across * 4 + dest},
+                conv_s.at[tile], conv_r.at[tile], {"dp": across * 4 + dest},
             ).start()
 
         each(4, send_conv)
 
+    take(do.at[chips], ag_r.at[0])
+    kt[...] = qkv[1].astype(F32).T.astype(BF)
+    grad = do[...]
+    dom[0] = jnp.where(first, grad, jnp.zeros_like(grad))
+    dom[1] = jnp.where(first, jnp.zeros_like(grad), grad)
+    dq_acc[...] = jnp.zeros_like(dq_acc)
+    product = ot[...].astype(F32) * grad.astype(F32).T
+    for h in range(2):
+        part = jnp.sum(product[h * HEAD_DIM : (h + 1) * HEAD_DIM], axis=0, keepdims=True)
+        delta[h] = jnp.broadcast_to(part, (SLAB, TOKENS))
+
+    def backward(i, carry):
+        here = rows(i, BLOCK)
+        key_grad = None
+        for h in range(2):
+            head = slice(h * HEAD_DIM, (h + 1) * HEAD_DIM)
+            prob = probs[h, here, :]
+            value_part = mm(prob, dom[h])
+            prob_grad = mm_nt(qkv[2, here, :], dom[h])
+            score_grad = (prob.astype(F32) * (prob_grad - delta[h, 0:1, :])).astype(BF)
+            key_part = mm(score_grad, qm[h])
+            dq_acc[head, :] += mm(kt[head, here], score_grad)
+            key_grad = key_part if key_grad is None else key_grad + key_part
+            value_grad = value_part if h == 0 else value_grad + value_part
+        gh[1, here, :] = key_grad.astype(BF)
+        gh[2, here, :] = value_grad.astype(BF)
+        for quarter_of in range(4):
+            peer = 4 * i + quarter_of
+
+            @pl.when(peer != s)
+            def _():
+                remote(
+                    gh.at[pl.ds(1, 2), rows(peer, HERE), :],
+                    grads_ref.at[pl.ds(1, 2), k, :, lanes(c)],
+                    gr_s.at[0], gr_r.at[0], {"space": peer},
+                ).start()
+
+        return carry
+
+    lax.fori_loop(0, 2, backward, 0)
+    sum_ow(0, along)
+    send_ow_on(0, by_z)
+    sum_ow(1, z)
+    send_ow_on(1, by_x)
+    lax.fori_loop(2, TOKENS // BLOCK, backward, 0)
+    gh[0] = (dq_acc[...] * SCALE).T.astype(BF)
+
+    def send_query(i):
+        peer = to(i)
+        remote(
+            gh.at[0, rows(peer, HERE), :], grads_ref.at[0, k, :, lanes(c)],
+            gq_s.at[0], gq_r.at[0], {"space": peer},
+        ).start()
+
+    each(SPACE, send_query)
+    own_grads = pltpu.make_async_copy(
+        gh.at[:, rows(s, HERE), :], grads_ref.at[:, k, :, lanes(c)], loc.at[0]
+    )
+    own_grads.start()
+
     opposite = {"dp": lax.rem(d + 4, DP)}
-    each(4, lambda i: take(ow_recv.at[i], ow_r.at[i]))
-    total = ow_send[rows(along, PAIR), :].astype(F32)
-    for i in range(1, 4):
-        total = total + ow_recv[i].astype(F32)
-    ow_keep[...] = total
-    ow_out[...] = ow_keep[rows(1 - across, HERE), :].astype(BF)
-    ow_turn = remote(ow_out, ow_back, oy_s.at[0], oy_r.at[0], opposite)
-    ow_turn.start()
-
     turns = []
     for tile, (at, end) in enumerate(tiles):
-        each(4, lambda i: take(conv_recv.at[i, :, :, at:end], conv_r.at[tile, i]))
+        take(conv_recv.at[pl.ds(1, 3), :, :, at:end], conv_r.at[tile])
         for half in range(2):
             total = conv_send[along, half, :, at:end].astype(F32)
             for i in range(1, 4):
@@ -488,17 +559,18 @@
         turn.start()
         turns.append(turn)
 
-    ow_turn.wait()
-    ow_sum[...] = ow_keep[rows(across, HERE), :] + ow_back[...].astype(F32)
-
-    def send_sum(i):
-        chip = chip_to(i)
+    sum_ow_on(0, z)
+    sum_ow_on(1, along)
+    place = across * 2 + column_y
+
+    def send_ow_y(i):
+        dest = lax.rem(place + i, 4)
         remote(
-            ow_sum.at[rows(chip, SLAB)], ow_parts.at[i],
-            sum_s.at[i], sum_r.at[i], {"space": chip * 2 + k},
+            ow_y.at[rows(dest, SLAB)], ow_parts.at[i], oy_s.at[0], oy_r.at[0],
+            {"dp": lax.div(dest, 2) * 4 + along, "space": (z * 2 + lax.rem(dest, 2)) * 2 + k},
         ).start()
 
-    each(CHIPS, send_sum)
+    each(4, send_ow_y)
 
     for tile, (at, end) in enumerate(tiles):
         turns[tile].wait()
@@ -506,42 +578,36 @@
         for tap in range(TAPS):
             gc_ref[tap, :, at:end] = total[tap * SLAB : (tap + 1) * SLAB]
 
-    each(CHIPS, lambda i: take(ow_parts.at[i], sum_r.at[i]))
-    total = ow_sum[rows(c, SLAB), :]
-    for i in range(1, CHIPS):
+    take(ow_parts.at[pl.ds(1, 3)], oy_r.at[0])
+    total = ow_y[rows(place, SLAB), :]
+    for i in range(1, 4):
         total = total + ow_parts[i]
     gw_ref[...] = total
 
     own_grads.wait()
 
-    def take_grads(i):
-        peer = frm(i)
-        take(grads_ref.at[:, lax.rem(peer, 2), :, lanes(lax.div(peer, 2))], gr_r.at[i])
-
-    each(SPACE, take_grads)
-
-    def sent(i):
-        take(qkv.at[:, rows(0, HERE), :], qkv_s.at[i])
-        take(hsend.at[rows(0, OWN)], hid_s.at[i])
-        take(gh.at[:, rows(0, HERE), :], gr_s.at[i])
-
-    each(SPACE, sent)
-
-    def sent_chips(i):
-        take(att.at[rows(0, PAIR)], att_s.at[chip_to(i)])
-        take(ag_tok.at[:, lanes(0)], ag_s.at[i])
-        take(ow_sum.at[rows(0, SLAB)], sum_s.at[i])
-
-    each(CHIPS, sent_chips)
-
-    def sent_along(i):
-        take(ow_send.at[rows(0, PAIR)], ow_s.at[i])
-        for tile, (at, end) in enumerate(tiles):
-            take(conv_send.at[0, :, :, at:end], conv_s.at[tile, i])
-
-    each(4, sent_along)
+    take(gh.at[pl.ds(1, 2), most], gr_r.at[0])
+    take(gh.at[0, most], gq_r.at[0])
+    take(qkv.at[pl.ds(0, 2), most], qkv_s.at[0])
+    take(qkv.at[2, most], qkv_s.at[1])
+    take(hsend.at[most], hid_s.at[0])
+    take(gh.at[pl.ds(1, 2), most], gr_s.at[0])
+    take(gh.at[0, most], gq_s.at[0])
+    take(att.at[chips], att_s.at[0])
+    take(do.at[chips], ag_s.at[0])
+    for path in range(2):
+        take(ow_recv.at[path, pl.ds(1, 3)], ow_s.at[path])
+        take(ow_xr.at[path, pl.ds(1, 3)], ox_s.at[path])
+    take(ow_parts.at[pl.ds(1, 3)], oy_s.at[0])
+    for tile, (at, end) in enumerate(tiles):
+        take(conv_recv.at[pl.ds(1, 3), :, :, at:end], conv_s.at[tile])
     for copy in ring:
         copy.wait_send()
+    take(six, share_s.at[0])
+    take(two, share_s.at[1])
+    for i in range(1, 5):
+        for core in range(2):
+            take(small, cot_s.at[i, core])
     for core in range(2):
         take(small, near_s.at[core, 1])
     take(small, near_s.at[1 - k, 0])
@@ -592,7 +658,7 @@
             pltpu.VMEM((2, TOKENS, PAIR), BF),
             pltpu.VMEM((PAIR, TOKENS), BF),
             pltpu.VMEM((PAIR, TOKENS), BF),
-            pltpu.VMEM((2, TOKENS, TOKENS), F32),
+            pltpu.VMEM((2, TOKENS, TOKENS), BF),
             pltpu.VMEM((PAIR, TOKENS), BF),
             pltpu.VMEM((TOKENS, PAIR), BF),
             pltpu.VMEM((PAIR, CH), BF),
@@ -608,34 +674,37 @@
             pltpu.VMEM((ROWS, COUT), BF),
             pltpu.VMEM((ROWS, COUT), BF),
             pltpu.VMEM((TOKENS, PAIR), BF),
-            pltpu.VMEM((TOKENS, PAIR), F32),
-            pltpu.VMEM((TOKENS, PAIR), F32),
+            pltpu.VMEM((2, SLAB, TOKENS), F32),
+            pltpu.VMEM((PAIR, TOKENS), F32),
             pltpu.VMEM((3, TOKENS, PAIR), BF),
-            pltpu.VMEM((2, CH // 2, PAIR), BF),
-            pltpu.VMEM((CH // 2, CH), BF),
-            pltpu.VMEM((CH // 2, CH), BF),
-            pltpu.VMEM((CH // 2, CH), BF),
-            pltpu.VMEM((4, PAIR, CH), BF),
-            pltpu.VMEM((PAIR, CH), F32),
-            pltpu.VMEM((HERE, CH), BF),
-            pltpu.VMEM((HERE, CH), BF),
-            pltpu.VMEM((HERE, CH), F32),
-            pltpu.VMEM((CHIPS, SLAB, CH), F32),
+            pltpu.VMEM((2, 2, HALF, PAIR), BF),
+            pltpu.VMEM((2, HALF, HALF), BF),
+            pltpu.VMEM((2, HALF, HALF), BF),
+            pltpu.VMEM((2, HALF, HALF), BF),
+            pltpu.VMEM((2, 4, PAIR, HALF), BF),
+            pltpu.VMEM((2, PAIR, HALF), F32),
+            pltpu.VMEM((2, PAIR, HALF), BF),
+            pltpu.VMEM((2, 4, GRID, HALF), BF),
+            pltpu.VMEM((GRID, CH), F32),
+            pltpu.VMEM((4, SLAB, CH), F32),
             sems((8,)),
             sems((3,)), sems((3,)),
-            sems((SPACE,)), sems((SPACE,)),
+            sems((2,)), sems((2,)),
             sems((2, 2)), sems((2, 2)),
-            sems((4,)), sems((4,)),
-            sems((CHIPS,)), sems((CHIPS,)),
-            sems((CHIPS,)), sems((CHIPS,)),
-            sems((SPACE,)), sems((SPACE,)),
-            sems((3, 4)), sems((3, 4)),
+            sems((5, 2)), sems((5, 2)),
+            sems((2,)), sems((2,)),
+            sems((2,)), sems((2,)),
+            sems((1,)), sems((1,)),
+            sems((1,)), sems((1,)),
+            sems((1,)), sems((1,)),
             sems((3,)), sems((3,)),
-            sems((4,)), sems((4,)),
+            sems((3,)), sems((3,)),
+            sems((2,)), sems((2,)),
+            sems((2,)), sems((2,)),
             sems((1,)), sems((1,)),
-            sems((CHIPS,)), sems((CHIPS,)),
-            sems((SPACE,)), sems((SPACE,)),
-            sems((2,)), sems((2,)),
+            sems((1,)), sems((1,)),
+            sems((1,)), sems((1,)),
+            sems((1,)), sems((1,)),
         ],
         compiler_params=pltpu.CompilerParams(
             collective_id=0, has_side_effects=True, vmem_limit_bytes=60 * 1024 * 1024

time: 76.9 us -> 70.4 us (0.915)
  Pallas kernels: 76.1 us -> 69.6 us
    pallas_call x1, Pallas kernels: 74.2 us -> 67.6 us  [on_device(): pl.pallas_call(kernel, out_shape=(jax.ShapeDtypeStruct((3, 2, HERE, CH),...]
where the time goes in v3:
time: 70.4 us; the launch traced here: 70.2 us
  Pallas kernels  69.6 us (99%)
    pallas_call x1, Pallas kernels, on_device(): pl.pallas_call(kernel, out_shape=(jax.ShapeDtypeStruct((3, 2, HERE, CH),...  67.6 us
    pallas_call x1, Pallas kernels, on_device(): pl.pallas_call(hand_over, out_shape=(wide, wide, wide, gw_shape, gc_shape...  1.98 us

profile of v3, /device:TPU:0, one launch (start us, length us, event | category | flops | bytes accessed | tf_op | source)
XLA Modules:
  0.0 70.2 jit_solution(5523589147465193736)
XLA Ops:
  0.6 67.6 %shard_map.119 = (bf16[3,2,64,1024]{3,2,1,0:T(8,128)(2,1)}, f32[8,1024]{1,0:T(8,128)}, f32[9,8,640]{2,1,0:T(8,128)}) custom-call(bf16[2,64,1024]{2,1,0:T(8,128)(2,1)} %q_ref.1, bf16[2,64,1024]{2,1,0:T(8,128)(2,1)} %k_ref.1, bf16[2,64,1024]{2,1,0:T(8,128)(2,1)} %v_ref.1, bf16[2,64,640]{2,1,0:T(8,128)(2,1)} %cot_ref.1, bf16[1024,1024]{1,0:T(8,128)(2,1)} %w_ref.1, ...), custom_call_target="tpu_custom_call" | custom-call | flops 8000000000 | bytes 20000000 | tf_op jit(solution)/shard_map/pallas_call | solution.py:643
  68.2 2.0 %shard_map.120 = (bf16[2,64,1024]{2,1,0:T(8,128)(2,1)}, bf16[2,64,1024]{2,1,0:T(8,128)(2,1)}, bf16[2,64,1024]{2,1,0:T(8,128)(2,1)}, f32[8,1024]{1,0:T(8,128)}, f32[9,8,640]{2,1,0:T(8,128)}) custom-call(bf16[3,2,64,1024]{3,2,1,0:T(8,128)(2,1)} %get-tuple-element.13.refs_0_, f32[8,1024]{1,0:T(8,128)} %get-tuple-element.14.refs_1_, ...), custom_call_target="tpu_custom_call" | custom-call | tf_op jit(solution)/shard_map/pallas_call | solution.py:719

commit v4 on v3

--- a/solution.py
+++ b/solution.py
@@ -522,12 +522,12 @@
 
         return carry
 
-    lax.fori_loop(0, 2, backward, 0)
+    lax.fori_loop(0, 3, backward, 0)
     sum_ow(0, along)
     send_ow_on(0, by_z)
     sum_ow(1, z)
     send_ow_on(1, by_x)
-    lax.fori_loop(2, TOKENS // BLOCK, backward, 0)
+    lax.fori_loop(3, TOKENS // BLOCK, backward, 0)
     gh[0] = (dq_acc[...] * SCALE).T.astype(BF)
 
     def send_query(i):

time: 70.4 us -> 70.8 us (level)
  no operation moved by 1% of the time
where the time goes in v4:
time: 70.8 us; the launch traced here: 70.2 us
  Pallas kernels  69.6 us (98%)
    pallas_call x1, Pallas kernels, on_device(): pl.pallas_call(kernel, out_shape=(jax.ShapeDtypeStruct((3, 2, HERE, CH),...  67.6 us
    pallas_call x1, Pallas kernels, on_device(): pl.pallas_call(hand_over, out_shape=(wide, wide, wide, gw_shape, gc_shape...  1.98 us

profile of v4, /device:TPU:0, one launch (start us, length us, event | category | flops | bytes accessed | tf_op | source)
XLA Modules:
  0.0 70.2 jit_solution(8413760198088807536)
XLA Ops:
  0.6 67.6 %shard_map.119 = (bf16[3,2,64,1024]{3,2,1,0:T(8,128)(2,1)}, f32[8,1024]{1,0:T(8,128)}, f32[9,8,640]{2,1,0:T(8,128)}) custom-call(bf16[2,64,1024]{2,1,0:T(8,128)(2,1)} %q_ref.1, bf16[2,64,1024]{2,1,0:T(8,128)(2,1)} %k_ref.1, bf16[2,64,1024]{2,1,0:T(8,128)(2,1)} %v_ref.1, bf16[2,64,640]{2,1,0:T(8,128)(2,1)} %cot_ref.1, bf16[1024,1024]{1,0:T(8,128)(2,1)} %w_ref.1, ...), custom_call_target="tpu_custom_call" | custom-call | flops 8000000000 | bytes 20000000 | tf_op jit(solution)/shard_map/pallas_call | solution.py:643
  68.2 2.0 %shard_map.120 = (bf16[2,64,1024]{2,1,0:T(8,128)(2,1)}, bf16[2,64,1024]{2,1,0:T(8,128)(2,1)}, bf16[2,64,1024]{2,1,0:T(8,128)(2,1)}, f32[8,1024]{1,0:T(8,128)}, f32[9,8,640]{2,1,0:T(8,128)}) custom-call(bf16[3,2,64,1024]{3,2,1,0:T(8,128)(2,1)} %get-tuple-element.13.refs_0_, f32[8,1024]{1,0:T(8,128)} %get-tuple-element.14.refs_1_, ...), custom_call_target="tpu_custom_call" | custom-call | tf_op jit(solution)/shard_map/pallas_call | solution.py:719
